TPU v7x, 512 devices: a whole 4x8x8 slice. The times are simulated.
512 devices in a mesh: hi: 16 (over z_lo, y), lo: 32 (over z_hi, x, core).
Axes of the slice: x: 4, y: 8, z: 8 (z_hi: 4, z_lo: 2; z = z_hi * 2 + z_lo), core: 2. Of those that a mesh axis runs over, the one named last changes fastest.
Arguments:
- state: float32 [16, 32, 262144], P('hi', 'lo'), may hold values from -6 to 6
- layer_angles: float32 [2, 2, 3, 6], replicated, may hold values from -3.140625 to 3.140625
- global_angles: float32 [2], replicated, may hold values from -3.140625 to 3.140625
Outputs:
- final_state: float32 [16, 32, 262144], P('hi', 'lo')
All inputs are finite; a program needn't handle non-finite values.
Results may differ from a plain program's by a relative error of at most 0.00012.
Values sent between devices are 32-bit elements; how exact they have to be, the bound alone decides.
No kernel may reach another device: no remote copies, remote signals or barrier semaphores. Data moves between devices by JAX's collectives and lax.ppermute only.
A program may use at most 64 MiB of HBM per device.

v0:
```python
import jax
import jax.numpy as jnp
from jax import lax
from jax.sharding import PartitionSpec as P

QB = 6
DEPTH = 2
G = 64


def partner_2(array, axis, distance):
    return lax.ppermute(array, axis, [(i, i ^ 1 << distance) for i in range(lax.axis_size(axis))])


def merged_gates(angles):
    row_ids = jnp.arange(G, dtype=jnp.int32)
    cosines = jnp.cos(angles * 0.5)
    sines = jnp.sin(angles * 0.5)
    result = jnp.ones((3, G, G), dtype=angles.dtype)
    ladder = jnp.zeros((G,), dtype=jnp.int32)
    for qubit in range(QB):
        row_bit = row_ids // 2 ** (QB - 1 - qubit) % 2
        left_bit = row_bit[:, None]
        right_bit = row_bit[None, :]
        signed = jnp.where(left_bit == 1, 1.0, -1.0).astype(angles.dtype)
        entry = jnp.where(
            (left_bit == right_bit)[None],
            cosines[:, qubit][:, None, None],
            signed[None] * sines[:, qubit][:, None, None],
        )
        result = result * entry
        if qubit + 1 < QB:
            next_bit = row_ids // 2 ** (QB - 2 - qubit) % 2
            ladder = ladder + row_bit * next_bit
    parity = (1 - 2 * (ladder % 2)).astype(angles.dtype)
    return result * parity[None, :, None]


def cross_signs(dtype):
    row_ids = jnp.arange(G, dtype=jnp.int32)
    low_bit = row_ids % 2
    high_bit = row_ids // (G // 2)
    count = (
        low_bit[:, None, None] * high_bit[None, :, None]
        + low_bit[None, :, None] * high_bit[None, None, :]
    )
    return (1 - 2 * (count % 2)).astype(dtype)


def apply_section(amps, section_angles):
    ladder = cross_signs(amps.dtype)
    identity_two = jnp.eye(2, dtype=amps.dtype)
    for layer in range(DEPTH):
        gates = merged_gates(section_angles[layer])
        amps = jnp.dot(
            gates[0],
            amps.reshape(G, G * G),
            precision=lax.Precision.HIGHEST,
            preferred_element_type=jnp.float32,
        )
        swapped = amps.reshape(G, G, G).transpose(1, 0, 2).reshape(G, G * G)
        swapped = jnp.dot(
            gates[1], swapped, precision=lax.Precision.HIGHEST, preferred_element_type=jnp.float32
        )
        widened = jnp.kron(identity_two, gates[2])
        swapped = jnp.dot(
            swapped.reshape(G * G // 2, 2 * G),
            widened.T,
            precision=lax.Precision.HIGHEST,
            preferred_element_type=jnp.float32,
        )
        amps = swapped.reshape(G, G, G).transpose(1, 0, 2)
        amps = amps * ladder
    return amps


def combine_pair(own, partner, angle, bit, hi_index):
    own_bit = hi_index // 2**bit % 2
    sign_factor = (2 * own_bit - 1).astype(own.dtype)
    return jnp.cos(angle * 0.5) * own + sign_factor * jnp.sin(angle * 0.5) * partner


def on_device(state, layer_angles, global_angles):
    full_shape = state.shape
    amps = state.reshape(G, G, G)
    hi_index = lax.axis_index("hi")
    upper_bit = lax.axis_size("hi").bit_length() - 2
    lo_count = lax.axis_size("lo")
    amps = apply_section(amps, layer_angles[0])
    partner = partner_2(amps, "hi", 0)
    amps = combine_pair(amps, partner, global_angles[0], 0, hi_index)
    moved = lax.all_to_all(
        amps.reshape(lo_count, -1), "lo", split_axis=0, concat_axis=0, tiled=True
    )
    amps = moved.reshape(G, G, G)
    amps = apply_section(amps, layer_angles[1])
    partner = partner_2(amps, "hi", upper_bit)
    amps = combine_pair(amps, partner, global_angles[1], upper_bit, hi_index)
    return amps.reshape(full_shape)


def solution(mesh):
    return jax.shard_map(
        on_device,
        mesh=mesh,
        in_specs=(P("hi", "lo", None), P(), P()),
        out_specs=P("hi", "lo", None),
        check_vma=False,
    )
```

profile of v0, /device:TPU:1, one launch (start us, length us, event | category | flops | bytes accessed | tf_op | source)
XLA Modules:
  0.0 252.9 jit_solution(18010669899431322858)
XLA Ops:
  0.2 1.0 fusion.19
  7.8 9.5 %reduce.100 = f32[262144]{0:T(1024)S(1)} reduce(f32[1,1,262144]{2,1,0:T(1,128)S(1)} %copy-done, f32[]{:T(128)} %broadcast.2153), dimensions={0,1}, to_apply=%param.3.reduce_sub_computation.3 | reduce | bytes 2097156 | tf_op args[0]
  18.1 8.2 %convolution_bitcast_fusion.3 = f32[64,64,64]{2,1,0:T(8,128)} fusion(f32[64,64,64]{2,1,0:T(8,128)S(1)} %bitcast.100, f32[3,64,64]{2,1,0:T(8,128)} %copy-done.4), kind=kOutput, calls=%fused_computation.18 | convolution fusion | flops 201326592 | bytes 2129920 | tf_op jit(solution)/shard_map/dot_general | solution.py:55
  26.3 2.1 reshape.1668
  28.4 1.8 fusion.4
  30.4 1.8 fusion.27
  32.6 3.3 %bitcast_multiply_fusion.3 = f32[64,64,64]{2,1,0:T(8,128)} fusion(f32[64,64,64]{2,1,0:T(8,128)S(1)} %reshape.1670, s32[64,64]{1,0:T(8,128)S(1)} %broadcast_multiply_fusion.4), kind=kLoop, calls=%fused_computation.12 | loop fusion | flops 4194304 | bytes 2113536 | tf_op jit(solution)/shard_map/mul | solution.py:73
  35.9 2.1 reshape.1671
  38.6 8.2 %convolution_bitcast_fusion.2 = f32[64,64,64]{2,1,0:T(8,128)} fusion(f32[64,64,64]{2,1,0:T(8,128)S(1)} %bitcast.101, f32[3,64,64]{2,1,0:T(8,128)} %copy-done.3), kind=kOutput, calls=%fused_computation.17 | convolution fusion | flops 201326592 | bytes 2129920 | tf_op jit(solution)/shard_map/dot_general | solution.py:55
  46.8 2.1 reshape.1672
  48.9 1.8 fusion.5
  50.9 1.8 fusion.28
  53.1 3.1 %bitcast_multiply_fusion.2 = f32[64,64,64]{2,1,0:T(8,128)} fusion(f32[64,64,64]{2,1,0:T(8,128)S(1)} %reshape.1674, s32[64,64]{1,0:T(8,128)S(1)} %broadcast_multiply_fusion.4), kind=kLoop, calls=%fused_computation.11 | loop fusion | flops 4194304 | bytes 2113536 | tf_op jit(solution)/shard_map/mul | solution.py:73
  56.2 4.0 %collective-permute-start = (f32[64,64,64]{2,1,0:T(8,128)}, f32[64,64,64]{2,1,0:T(8,128)}, u32[]{:S(2)}, u32[]{:S(2)}) collective-permute-start(f32[64,64,64]{2,1,0:T(8,128)} %bitcast_multiply_fusion.2), channel_id=1, source_target_pairs={{0,32},{32,0},{64,96},{96,64},{128,160},{160,128},{192,224},{224,1... | collective-permute-start | bytes 3145736 | tf_op jit(solution)/shard_map/ppermute | solution.py:12
  61.6 39.3 %collective-permute-done = f32[64,64,64]{2,1,0:T(8,128)} collective-permute-done((f32[64,64,64]{2,1,0:T(8,128)}, f32[64,64,64]{2,1,0:T(8,128)}, u32[]{:S(2)}, u32[]{:S(2)}) %collective-permute-start) | collective-permute-done | bytes 1048608 | tf_op jit(solution)/shard_map/ppermute | solution.py:12
  100.9 4.9 %multiply_add_fusion.1 = f32[64,64,64]{2,1,0:T(8,128)} fusion(f32[64,64,64]{2,1,0:T(8,128)} %collective-permute-done, f32[]{:T(128)S(6)} %mul.961, f32[]{:T(128)} %bitcast.7, s32[64,64]{1,0:T(8,128)S(1)} %broadcast_multiply_fusion.4, f32[64,64,64]{2,1,0:T(8,128)S(1)} %reshape.1674), kind=kLoop, calls=%fused_computation.14 | loop fusion | flops 4980736 | bytes 3162120 | tf_op jit(solution)/shard_map/add | solution.py:80
  105.8 3.4 %all_to_all.8 = f32[32,1,8192]{2,1,0:T(1,128)} reshape(f32[64,64,64]{2,1,0:T(8,128)} %multiply_add_fusion.1) | data formatting | bytes 2097152 | tf_op jit(solution)/shard_map/all_to_all | solution.py:92
  109.2 19.8 %all-to-all-start = ((f32[32,1,8192]{2,1,0:T(1,128)}), f32[32,1,8192]{2,1,0:T(1,128)S(1)}, u32[]{:S(2)}, u32[]{:S(2)}) async-start(f32[32,1,8192]{2,1,0:T(1,128)} %all_to_all.8), calls=%async_computation | async-start | bytes 2097152 | tf_op jit(solution)/shard_map/all_to_all | solution.py:92
  129.8 23.1 %all-to-all-done = f32[32,1,8192]{2,1,0:T(1,128)S(1)} async-done(((f32[32,1,8192]{2,1,0:T(1,128)}), f32[32,1,8192]{2,1,0:T(1,128)S(1)}, u32[]{:S(2)}, u32[]{:S(2)}) %all-to-all-start) | async-done | bytes 1048608 | tf_op jit(solution)/shard_map/all_to_all | solution.py:92
  152.9 2.6 %reduce.49 = f32[32,8192]{1,0:T(8,128)S(1)} reduce(f32[32,1,8192]{2,1,0:T(1,128)S(1)} %all-to-all-done, f32[]{:T(128)} %constant.460), dimensions={1}, to_apply=%all_to_all.7.reduce_sub_computation | reduce | bytes 2097156 | tf_op jit(solution)/shard_map/all_to_all | solution.py:92
  156.3 7.4 %convolution_bitcast_fusion.1 = f32[64,64,64]{2,1,0:T(8,128)} fusion(f32[64,64,64]{2,1,0:T(8,128)S(1)} %bitcast.102, f32[3,64,64]{2,1,0:T(8,128)S(1)} %multiply_multiply_fusion.2), kind=kOutput, calls=%fused_computation.16 | convolution fusion | flops 201326592 | bytes 3178496 | tf_op jit(solution)/shard_map/dot_general | solution.py:55
  163.7 2.1 reshape.1675
  168.3 3.1 %bitcast_multiply_fusion.1 = f32[64,64,64]{2,1,0:T(8,128)} fusion(f32[64,64,64]{2,1,0:T(8,128)S(1)} %reshape.1677, s32[64,64]{1,0:T(8,128)S(1)} %broadcast_multiply_fusion.4), kind=kLoop, calls=%fused_computation.10 | loop fusion | flops 4194304 | bytes 2113536 | tf_op jit(solution)/shard_map/mul | solution.py:73
  171.4 2.3 reshape.1678
  174.6 7.4 %convolution_bitcast_fusion = f32[64,64,64]{2,1,0:T(8,128)} fusion(f32[64,64,64]{2,1,0:T(8,128)S(1)} %bitcast.103, f32[3,64,64]{2,1,0:T(8,128)S(1)} %copy-done.2), kind=kOutput, calls=%fused_computation.15 | convolution fusion | flops 201326592 | bytes 3178496 | tf_op jit(solution)/shard_map/dot_general | solution.py:55
  182.1 2.1 reshape.1679
  184.2 1.0 fusion.7
  186.7 3.1 %bitcast_multiply_fusion = f32[64,64,64]{2,1,0:T(8,128)} fusion(f32[64,64,64]{2,1,0:T(8,128)S(1)} %reshape.1681, s32[64,64]{1,0:T(8,128)S(1)} %broadcast_multiply_fusion.4), kind=kLoop, calls=%fused_computation.9 | loop fusion | flops 4194304 | bytes 2113536 | tf_op jit(solution)/shard_map/mul | solution.py:73
  189.8 8.5 %collective-permute-start.1 = (f32[64,64,64]{2,1,0:T(8,128)}, f32[64,64,64]{2,1,0:T(8,128)}, u32[]{:S(2)}, u32[]{:S(2)}) collective-permute-start(f32[64,64,64]{2,1,0:T(8,128)} %bitcast_multiply_fusion), channel_id=1, source_target_pairs={{0,256},{32,288},{64,320},{96,352},{128,384},{160,416},{192,448},{... | collective-permute-start | bytes 3145736 | tf_op jit(solution)/shard_map/ppermute | solution.py:12
  199.1 44.9 %collective-permute-done.1 = f32[64,64,64]{2,1,0:T(8,128)} collective-permute-done((f32[64,64,64]{2,1,0:T(8,128)}, f32[64,64,64]{2,1,0:T(8,128)}, u32[]{:S(2)}, u32[]{:S(2)}) %collective-permute-start.1) | collective-permute-done | bytes 1048608 | tf_op jit(solution)/shard_map/ppermute | solution.py:12
  244.0 4.9 %multiply_add_fusion = f32[64,64,64]{2,1,0:T(8,128)} fusion(f32[64,64,64]{2,1,0:T(8,128)} %collective-permute-done.1, f32[]{:T(128)S(6)} %mul.976, f32[]{:T(128)} %bitcast, s32[64,64]{1,0:T(8,128)S(1)} %broadcast_multiply_fusion.4, f32[64,64,64]{2,1,0:T(8,128)S(1)} %reshape.1681), kind=kLoop, calls=%fused_computation.13 | loop fusion | flops 4980736 | bytes 3162120 | tf_op jit(solution)/shard_map/add | solution.py:80
  248.8 3.9 %reshape.1682 = f32[1,1,262144]{2,1,0:T(1,128)} reshape(f32[64,64,64]{2,1,0:T(8,128)} %multiply_add_fusion) | data formatting | bytes 2097152 | tf_op jit(solution)/shard_map/reshape | solution.py:99
  (83 shorter events, 16.0 us)
Async XLA Ops:
  0.0 7.8 %copy-start = (f32[1,1,262144]{2,1,0:T(1,128)S(1)}, f32[1,1,262144]{2,1,0:T(1,128)}, u32[]{:S(2)}) copy-start(f32[1,1,262144]{2,1,0:T(1,128)} %param.3) | copy-start | bytes 3145732
  4.6 0.6 copy-start.3
  4.9 2.9 %copy-start.4 = (f32[3,64,64]{2,1,0:T(8,128)}, f32[3,64,64]{2,1,0:T(8,128)S(1)}, u32[]{:S(2)}) copy-start(f32[3,64,64]{2,1,0:T(8,128)S(1)} %multiply_multiply_fusion) | copy-start | bytes 147460
  5.5 2.3 copy-start.1
  53.1 7.1 %copy-start.6 = (f32[2]{0:T(128)S(1)}, f32[2]{0:T(128)}, u32[]{:S(2)}) copy-start(f32[2]{0:T(128)} %param.5) | copy-start | bytes 28
  56.2 44.8 %collective-permute-start = (f32[64,64,64]{2,1,0:T(8,128)}, f32[64,64,64]{2,1,0:T(8,128)}, u32[]{:S(2)}, u32[]{:S(2)}) collective-permute-start(f32[64,64,64]{2,1,0:T(8,128)} %bitcast_multiply_fusion.2), channel_id=1, source_target_pairs={{0,32},{32,0},{64,96},{96,64},{128,160},{160,128},{192,224},{224,1... | collective-permute-start | bytes 3145736 | tf_op jit(solution)/shard_map/ppermute | solution.py:12
  109.2 43.7 %all-to-all-start = ((f32[32,1,8192]{2,1,0:T(1,128)}), f32[32,1,8192]{2,1,0:T(1,128)S(1)}, u32[]{:S(2)}, u32[]{:S(2)}) async-start(f32[32,1,8192]{2,1,0:T(1,128)} %all_to_all.8), calls=%async_computation | async-start | bytes 2097152 | tf_op jit(solution)/shard_map/all_to_all | solution.py:92
  173.7 0.9 copy-start.2
  184.2 1.2 copy-start.5
  189.8 54.2 %collective-permute-start.1 = (f32[64,64,64]{2,1,0:T(8,128)}, f32[64,64,64]{2,1,0:T(8,128)}, u32[]{:S(2)}, u32[]{:S(2)}) collective-permute-start(f32[64,64,64]{2,1,0:T(8,128)} %bitcast_multiply_fusion), channel_id=1, source_target_pairs={{0,256},{32,288},{64,320},{96,352},{128,384},{160,416},{192,448},{... | collective-permute-start | bytes 3145736 | tf_op jit(solution)/shard_map/ppermute | solution.py:12
where the time goes:
time: 257 us; the launch traced here: 253 us
  waiting for transfers between devices  107 us (42%)
  matrix products  42.4 us (16%)
  other arithmetic  37.4 us (15%)
  starting transfers between devices  32.2 us (13%)
  local copies, waits for them, and re-layouts  31.2 us (12%)
    ppermute x2, waiting for transfers between devices, partner_2(): lax.ppermute(array, axis, [(i, i ^ 1 << distance) for i in range(lax.axis...  84.2 us
    dot_general x4, matrix products, apply_section(): jnp.dot(gates[0], amps.reshape(G, G * G), precision=lax.Precision.HIGHEST...  31.2 us
    all_to_all x1, waiting for transfers between devices, on_device(): lax.all_to_all(amps.reshape(lo_count, -1), 'lo', split_axis=0, concat_axi...  23.1 us
    all_to_all x1, starting transfers between devices, on_device(): lax.all_to_all(amps.reshape(lo_count, -1), 'lo', split_axis=0, concat_axi...  19.8 us
    mul x4, other arithmetic, apply_section(): amps = amps * ladder  12.6 us
    ppermute x2, starting transfers between devices, partner_2(): lax.ppermute(array, axis, [(i, i ^ 1 << distance) for i in range(lax.axis...  12.5 us
    add x2, other arithmetic, combine_pair(): jnp.cos(angle * 0.5) * own + sign_factor * jnp.sin(angle * 0.5) * partner  9.71 us
    unnamed x1, other arithmetic  9.49 us
  transfers between devices with their start and end apart: 3, of which 3 were waited for; matrix products, arithmetic and copies ran while one was open for 1% of the time, Pallas kernels for 0%

commit v1 on v0

v1 whole, which is shorter than its diff:
```python
import functools

import jax
import jax.numpy as jnp
from jax import lax
from jax.experimental import pallas as pl
from jax.experimental.pallas import tpu as pltpu
from jax.sharding import Mesh
from jax.sharding import PartitionSpec as P

ROW_BITS = (1, 2, 3, 4, 7, 8, 9, 10)
COL_BITS = (0, 11, 12, 13, 14, 15, 16, 17)
SIDE = 256
CHUNKS = 4
BLOCKS = 32
ROWS = 16
LANES = 128


def trig(angles_ref, section, layer):
    half = angles_ref[section, layer] * 0.5
    cosines, sines = jnp.cos(half), jnp.sin(half)

    def of(bit):
        group, qubit = bit // 6, bit % 6
        return (
            cosines[group : group + 1, qubit : qubit + 1],
            sines[group : group + 1, qubit : qubit + 1],
        )

    return of


def bit_of(index, place):
    return (index >> place) & 1


def gate_tiles(bits, of, transposed, skip=()):
    row = lax.broadcasted_iota(jnp.int32, (8, LANES), 0)
    lane = lax.broadcasted_iota(jnp.int32, (8, LANES), 1)
    pairs = [
        (i, i + 1)
        for i in range(7)
        if bits[i] + 1 == bits[i + 1] and not {bits[i], bits[i + 1]} & set(skip)
    ]

    def entry(bit, r, c):
        if bit in skip:
            if isinstance(r, int) and isinstance(c, int):
                return 1.0 if r == c else 0.0
            return jnp.where(r == c, 1.0, 0.0)
        cosine, sine = of(bit)
        out, inner = (c, r) if transposed else (r, c)
        if isinstance(r, int) and isinstance(c, int):
            return cosine if out == inner else sine if out == 1 else -sine
        return jnp.where(r == c, cosine, jnp.where(out == 1, sine, -sine))

    base = jnp.ones((8, LANES), jnp.float32)
    for i in (5, 6, 7):
        base = base * entry(bits[i], bit_of(row, 7 - i), bit_of(lane, 7 - i))
    out_bit = {i: bit_of(lane if transposed else row, 7 - i) for i in (range(1, 8) if transposed else range(5, 8))}
    parity = jnp.zeros((8, LANES), jnp.int32)
    for i, j in pairs:
        if i in out_bit and j in out_bit:
            parity = parity + out_bit[i] * out_bit[j]
    base = base * (1 - 2 * (parity & 1)).astype(jnp.float32)
    tiles = {(): base}
    for i in (4, 3, 2, 1):
        grown = {}
        for r in (0, 1):
            factor = entry(bits[i], r, bit_of(lane, 7 - i))
            if not transposed and r == 1 and (i, i + 1) in pairs and i + 1 in out_bit:
                factor = factor * (1 - 2 * out_bit[i + 1]).astype(jnp.float32)
            for key, tile in tiles.items():
                grown[(r, *key)] = tile * factor
        tiles = grown
    halves = []
    for c in (0, 1):
        column = {}
        for r in (0, 1):
            factor = entry(bits[0], r, c)
            if transposed and c == 1 and (0, 1) in pairs:
                factor = factor * (1 - 2 * out_bit[1]).astype(jnp.float32)
            for key, tile in tiles.items():
                column[(r, *key)] = tile * factor
        if not transposed:
            for key in column:
                flips = sum(key[i] * key[j] for i, j in pairs if i < 5 and j < 5)
                if flips % 2:
                    column[key] = -column[key]
        halves.append(jnp.concatenate([column[key] for key in sorted(column)], axis=0))
    return jnp.concatenate(halves, axis=1)


def split(value):
    high = value.astype(jnp.bfloat16)
    low = (value - high.astype(jnp.float32)).astype(jnp.bfloat16)
    return high, low


def dot3(left, right):
    mul = functools.partial(jnp.dot, preferred_element_type=jnp.float32)
    return mul(left[0], right[0]) + mul(left[0], right[1]) + mul(left[1], right[0])


def chunk_gates(angles_ref, section):
    first, later = trig(angles_ref, section, 0), trig(angles_ref, section, 1)
    return (
        split(gate_tiles(ROW_BITS, first, False)),
        split(gate_tiles(COL_BITS, first, True)),
        split(gate_tiles(ROW_BITS, later, False, skip=(4, 7))),
        split(gate_tiles(COL_BITS, later, True)),
    )


def cross_sign():
    row = lax.broadcasted_iota(jnp.int32, (SIDE, SIDE), 0)
    column = lax.broadcasted_iota(jnp.int32, (SIDE, SIDE), 1)
    parity = bit_of(row, 7) * bit_of(column, 7) + bit_of(row, 0) * bit_of(column, 6)
    return (1 - 2 * (parity & 1)).astype(jnp.float32)


def chunk_layers(chunk, gates, sign):
    left0, right0, left1, right1 = gates
    chunk = dot3(split(chunk), right0)
    chunk = dot3(left0, split(chunk)) * sign
    chunk = dot3(split(chunk), right1)
    return dot3(left1, split(chunk)) * sign


def finish_section(angles_ref, section, load, store):
    first, later = trig(angles_ref, section, 0), trig(angles_ref, section, 1)
    wide = lambda pair: tuple(jnp.broadcast_to(v, (8, LANES)) for v in pair)
    first = {bit: wide(first(bit)) for bit in (5, 6)}
    later = {bit: wide(later(bit)) for bit in (4, 5, 6, 7)}
    row = lax.broadcasted_iota(jnp.int32, (8, LANES), 0)
    flip8 = (1 - 2 * bit_of(row, 2)).astype(jnp.float32)

    def rotate(tiles, signs, place, pair):
        cosine, sine = pair
        for key in list(tiles):
            if key[place]:
                continue
            other = (*key[:place], 1, *key[place + 1 :])
            x, y = tiles[key], tiles[other]
            if signs[key] == signs[other]:
                tiles[key], tiles[other] = cosine * x - sine * y, sine * x + cosine * y
            else:
                tiles[key], tiles[other] = cosine * x + sine * y, sine * x - cosine * y
            signs[other] = signs[key]

    def group(base, b3):
        keys = [(b4, b5, b6, b7) for b4 in (0, 1) for b5 in (0, 1) for b6 in (0, 1) for b7 in (0, 1)]
        tiles = {key: load(key[1] * 2 + key[2], base + key[0], key[3]) for key in keys}
        signs = dict.fromkeys(keys, 1)
        rotate(tiles, signs, 1, first[5])
        rotate(tiles, signs, 2, first[6])
        for key in keys:
            b4, b5, b6, b7 = key
            signs[key] *= (-1) ** (b4 * b5 + b5 * b6 + b6 * b7)
        for place, bit in enumerate((4, 5, 6, 7)):
            rotate(tiles, signs, place, later[bit])
        for key in keys:
            b4, b5, b6, b7 = key
            sign = signs[key] * (-1) ** (b3 * b4 + b4 * b5 + b5 * b6 + b6 * b7)
            value = tiles[key]
            if b7:
                value = value * (flip8 if sign == 1 else -flip8)
            elif sign == -1:
                value = -value
            store(b5 * 2 + b6, base + b4, b7, value)

    @pl.loop(0, 8)
    def _(step):
        group(step * 4, 0)
        group(step * 4 + 2, 1)


def half_rows(b7):
    return pl.ds(b7 * 8, 8)


def first_kernel(angles_ref, state_ref, out_ref):
    gates = chunk_gates(angles_ref, 0)
    sign = cross_sign()
    for c in range(CHUNKS):
        chunk = jnp.concatenate(
            [state_ref[half * 16 : half * 16 + 16, c].reshape(SIDE, LANES) for half in (0, 1)], axis=1
        )
        chunk = chunk_layers(chunk, gates, sign)
        for half in (0, 1):
            out_ref[c, half * 16 : half * 16 + 16] = chunk[:, half * LANES : (half + 1) * LANES].reshape(16, ROWS, LANES)

    def load(c, block, b7):
        return out_ref[c, block, half_rows(b7)]

    def store(c, block, b7, value):
        out_ref[c, block, half_rows(b7)] = value

    finish_section(angles_ref, 0, load, store)


def middle_kernel(angles_ref, global_ref, in_ref, out_ref):
    gates = chunk_gates(angles_ref, 1)
    sign = cross_sign()
    half = global_ref[...] * 0.5
    cosines, sines = jnp.cos(half), jnp.sin(half)
    low, high = ((cosines[:, i : i + 1], sines[:, i : i + 1]) for i in (0, 1))

    def entry(pair, out, inner):
        return pair[0] if out == inner else pair[1] if out == 1 else -pair[1]

    for c in range(CHUNKS):
        halves = []
        for side in (0, 1):
            total = None
            for source in range(CHUNKS):
                factor = entry(high, c >> 1, source >> 1) * entry(low, c & 1, source & 1)
                term = factor * in_ref[source, side * 16 : side * 16 + 16].reshape(SIDE, LANES)
                total = term if total is None else total + term
            halves.append(total)
        chunk = chunk_layers(jnp.concatenate(halves, axis=1), gates, sign)
        for side in (0, 1):
            out_ref[c, side * 16 : side * 16 + 16] = chunk[:, side * LANES : (side + 1) * LANES].reshape(16, ROWS, LANES)


def last_kernel(angles_ref, in_ref, out_ref):
    def load(c, block, b7):
        return in_ref[c, block, half_rows(b7)]

    def store(c, block, b7, value):
        out_ref[block, c, half_rows(b7)] = value

    finish_section(angles_ref, 1, load, store)


VMEM = pl.BlockSpec(memory_space=pltpu.VMEM)


def call(kernel, shape, *args):
    return pl.pallas_call(
        kernel,
        out_shape=jax.ShapeDtypeStruct(shape, jnp.float32),
        in_specs=[VMEM] * len(args),
        out_specs=VMEM,
        compiler_params=pltpu.CompilerParams(vmem_limit_bytes=32 * 2**20),
    )(*args)


def on_device(state, layer_angles, global_angles):
    by_chunk = (CHUNKS, BLOCKS, ROWS, LANES)
    amps = call(first_kernel, by_chunk, layer_angles, state.reshape(BLOCKS, CHUNKS, ROWS, LANES))
    amps = lax.all_to_all(
        amps.reshape(CHUNKS * BLOCKS, ROWS, LANES), ("h3", "h0", "lo"), split_axis=0, concat_axis=0, tiled=True
    )
    amps = call(middle_kernel, by_chunk, layer_angles, global_angles.reshape(1, 2), amps.reshape(by_chunk))
    amps = lax.all_to_all(
        amps.reshape(CHUNKS, BLOCKS * ROWS, LANES), ("h3", "h0"), split_axis=0, concat_axis=0, tiled=True
    )
    amps = call(last_kernel, (BLOCKS, CHUNKS, ROWS, LANES), layer_angles, amps.reshape(by_chunk))
    return amps.reshape(state.shape)


def solution(mesh):
    high, low = mesh.shape["hi"], mesh.shape["lo"]
    finer = Mesh(mesh.devices.reshape(2, high // 4, 2, low), ("h3", "hm", "h0", "lo"))
    spec = P(("h3", "hm", "h0"), "lo", None)
    return jax.shard_map(on_device, mesh=finer, in_specs=(spec, P(), P()), out_specs=spec, check_vma=False)
```

time: 257 us -> 74.5 us (0.29)
  the two profiles are of different devices: /device:TPU:1 before, /device:TPU:16 now
where the time goes in v1:
time: 74.5 us; the launch traced here: 74.2 us
  blocking collectives  61.4 us (82%)
  Pallas kernels  10.2 us (14%)
  local copies, waits for them, and re-layouts  2.57 us (3%)
    all_to_all x1, blocking collectives, on_device(): lax.all_to_all(amps.reshape(CHUNKS * BLOCKS, ROWS, LANES), ('h3', 'h0', '...  44.2 us
    all_to_all x1, blocking collectives, on_device(): lax.all_to_all(amps.reshape(CHUNKS, BLOCKS * ROWS, LANES), ('h3', 'h0'),...  17.3 us
    pallas_call x3, Pallas kernels, call(): pl.pallas_call(kernel, out_shape=jax.ShapeDtypeStruct(shape, jnp.float32)...  10.2 us
    unnamed x5, local copies, waits for them, and re-layouts  2.57 us

profile of v1, /device:TPU:16, one launch (start us, length us, event | category | flops | bytes accessed | tf_op | source)
XLA Modules:
  0.0 74.2 jit_solution(4869985343632044153)
XLA Ops:
  0.0 0.7 copy.6.angles_ref
  0.7 0.0 copy-start
  0.7 1.2 %copy-done = f32[1,1,262144]{2,1,0:T(1,128)S(1)} copy-done((f32[1,1,262144]{2,1,0:T(1,128)S(1)}, f32[1,1,262144]{2,1,0:T(1,128)}, u32[]{:S(2)}) %copy-start) | copy-done | bytes 1048600
  1.9 4.5 %shard_map.37 = f32[4,32,16,128]{3,2,1,0:T(8,128)S(1)} custom-call(f32[2,2,3,6]{3,2,1,0:T(4,128)S(1)} %copy.6.angles_ref, f32[32,4,16,128]{3,2,1,0:T(8,128)S(1)} %bitcast.11), custom_call_target="tpu_custom_call" | custom-call | tf_op jit(solution)/shard_map/pallas_call | solution.py:241
  6.5 44.2 %all_to_all.10 = f32[128,16,128]{2,1,0:T(8,128)S(1)} all-to-all(f32[128,16,128]{2,1,0:T(8,128)S(1)} %bitcast.10), channel_id=1, replica_groups=mesh['h3'=2,'hm'=4,'h0'=2,'lo'=32] {'h3','h0','lo'}, dimensions={0} | all-to-all | bytes 2097152 | tf_op jit(solution)/shard_map/all_to_all | solution.py:253
  50.6 0.0 copy-start.1
  50.6 0.7 copy-done.1
  51.3 3.8 %shard_map.38 = f32[4,32,16,128]{3,2,1,0:T(8,128)S(1)} custom-call(f32[2,2,3,6]{3,2,1,0:T(4,128)S(1)} %copy.6.angles_ref, f32[1,2]{1,0:T(1,128)S(1)} %bitcast.12, f32[4,32,16,128]{3,2,1,0:T(8,128)S(1)} %bitcast.7), custom_call_target="tpu_custom_call" | custom-call | tf_op jit(solution)/shard_map/pallas_call | solution.py:241
  55.2 17.3 %all_to_all.11 = f32[4,512,128]{2,1,0:T(8,128)S(1)} all-to-all(f32[4,512,128]{2,1,0:T(8,128)S(1)} %bitcast.8), channel_id=1, replica_groups=mesh['h3'=2,'hm'=4,'h0'=2,'lo'=32] {'h3','h0'}, dimensions={0} | all-to-all | bytes 2097152 | tf_op jit(solution)/shard_map/all_to_all | solution.py:257
  72.4 1.8 %shard_map.39 = f32[32,4,16,128]{3,2,1,0:T(8,128)} custom-call(f32[2,2,3,6]{3,2,1,0:T(4,128)S(1)} %copy.6.angles_ref, f32[4,32,16,128]{3,2,1,0:T(8,128)S(1)} %bitcast.9), custom_call_target="tpu_custom_call" | custom-call | tf_op jit(solution)/shard_map/pallas_call | solution.py:241
Async XLA Ops:
  0.7 1.2 %copy-start = (f32[1,1,262144]{2,1,0:T(1,128)S(1)}, f32[1,1,262144]{2,1,0:T(1,128)}, u32[]{:S(2)}) copy-start(f32[1,1,262144]{2,1,0:T(1,128)} %param.3) | copy-start | bytes 3145732
  50.6 0.7 copy-start.1

commit v2 on v0

v2 whole, which is shorter than its diff:
```python
import functools

import jax
import jax.numpy as jnp
from jax import lax
from jax.experimental import pallas as pl
from jax.experimental.pallas import tpu as pltpu
from jax.sharding import Mesh
from jax.sharding import PartitionSpec as P

ROW_BITS = (1, 2, 3, 4, 7, 8, 9, 10)
COL_BITS = (0, 11, 12, 13, 14, 15, 16, 17)
SIDE = 256
CHUNKS = 4
BLOCKS = 32
ROWS = 16
LANES = 128
TILE = (8, LANES)
MIB = 2**20
PARTS = 4


def trig(angles_ref, section, layer):
    half = angles_ref[section, :, layer] * 0.5
    cosines, sines = jnp.cos(half), jnp.sin(half)

    def of(bit):
        group, qubit = bit // 6, bit % 6
        return (
            cosines[group : group + 1, qubit : qubit + 1],
            sines[group : group + 1, qubit : qubit + 1],
        )

    return of


def bit_of(index, place):
    return (index >> place) & 1


def signs_of(parity):
    return (1 - 2 * (parity & 1)).astype(jnp.float32)


def ry(pair, out, inner):
    cosine, sine = pair
    if isinstance(out, int):
        return cosine if out == inner else sine if out == 1 else -sine
    return jnp.where(out == inner, cosine, jnp.where(out == 1, sine, -sine))


def gate(bits, of, transposed):
    row = lax.broadcasted_iota(jnp.int32, TILE, 0)
    lane = lax.broadcasted_iota(jnp.int32, TILE, 1)
    pairs = [(i, i + 1) for i in range(7) if bits[i] + 1 == bits[i + 1]]

    def entry(i, r, c):
        cosine, sine = of(bits[i])
        out, inner = (c, r) if transposed else (r, c)
        if isinstance(c, int):
            return ry((cosine, sine), out, inner)
        return jnp.where(r == c, cosine, jnp.where(out == 1, sine, -sine))

    if transposed:
        out_bit = {i: bit_of(lane, 7 - i) for i in range(1, 8)}
    else:
        out_bit = {i: bit_of(row, 7 - i) for i in range(5, 8)}
    base = jnp.ones(TILE, jnp.float32)
    for i in (5, 6, 7):
        base = base * entry(i, bit_of(row, 7 - i), bit_of(lane, 7 - i))
    parity = jnp.zeros(TILE, jnp.int32)
    for i, j in pairs:
        if i in out_bit and j in out_bit:
            parity = parity + out_bit[i] * out_bit[j]
    tiles = {(): base * signs_of(parity)}
    for i in (4, 3, 2, 1):
        grown = {}
        for r in (0, 1):
            factor = entry(i, r, bit_of(lane, 7 - i))
            if not transposed and r == 1 and (i, i + 1) in pairs and i + 1 in out_bit:
                factor = factor * signs_of(out_bit[i + 1])
            for key, tile in tiles.items():
                grown[(r, *key)] = tile * factor
        tiles = grown
    halves = []
    for c in (0, 1):
        column = {}
        for r in (0, 1):
            factor = entry(0, r, c)
            if transposed and c == 1 and (0, 1) in pairs:
                factor = factor * signs_of(out_bit[1])
            for key, tile in tiles.items():
                column[(r, *key)] = tile * factor
        if not transposed:
            for key in column:
                if sum(key[i] * key[j] for i, j in pairs if j < 5) % 2:
                    column[key] = -column[key]
        halves.append(jnp.concatenate([column[key] for key in sorted(column)], axis=0))
    return jnp.concatenate(halves, axis=1)


def split(value):
    high = value.astype(jnp.bfloat16)
    low = (value - high.astype(jnp.float32)).astype(jnp.bfloat16)
    return high, low


def dot3(left, right):
    mul = functools.partial(jnp.dot, preferred_element_type=jnp.float32)
    return mul(left[0], right[0]) + mul(left[0], right[1]) + mul(left[1], right[0])


def section_gates(angles_ref, section):
    gates = []
    for layer in (0, 1):
        of = trig(angles_ref, section, layer)
        gates.append(split(gate(COL_BITS, of, True)))
        gates.append(split(gate(ROW_BITS, of, False)))
    return gates


def edge_tile():
    row = lax.broadcasted_iota(jnp.int32, TILE, 0)
    lane = lax.broadcasted_iota(jnp.int32, TILE, 1)
    return signs_of(bit_of(row, 0) * bit_of(lane, 6))


def chunk_sign(tile_of):
    tiles = {(b4, b7): tile_of(b4, b7) for b4 in (0, 1) for b7 in (0, 1)}
    columns = []
    for b0 in (0, 1):
        column = []
        for upper in range(16):
            for b7 in (0, 1):
                tile = tiles[upper & 1, b7]
                column.append(-tile if b0 and upper >= 8 else tile)
        columns.append(jnp.concatenate(column, axis=0))
    return jnp.concatenate(columns, axis=1)


def chunk_layers(chunks, gates, signs0, sign1):
    right0, left0, right1, left1 = gates
    chunks = [dot3(split(chunk), right0) for chunk in chunks]
    chunks = [dot3(left0, split(chunk)) * sign for chunk, sign in zip(chunks, signs0, strict=True)]
    chunks = [dot3(split(chunk), right1) for chunk in chunks]
    return [dot3(left1, split(chunk)) * sign1 for chunk in chunks]


def weighted(factors, values):
    total = None
    for factor, value in zip(factors, values, strict=True):
        term = factor * value
        total = term if total is None else total + term
    return total


def to_chunk(pieces):
    return jnp.concatenate([piece.reshape(SIDE, LANES) for piece in pieces], axis=1)


def of_chunk(chunk, half):
    return chunk[:, half * LANES : (half + 1) * LANES].reshape(16, ROWS, LANES)


def halves(half):
    return slice(half * 16, half * 16 + 16)


def outer_parity(b4, b5, b6, b7):
    return (b4 * b5 + b5 * b6 + b6 * b7) % 2


def first_kernel(angles_ref, state_ref, out_ref, angles, held, mixed, done):
    copies = [pltpu.make_async_copy(angles_ref, angles, done.at[PARTS])]
    for part in range(PARTS):
        span = pl.ds(part * BLOCKS // PARTS, BLOCKS // PARTS)
        copies.append(pltpu.make_async_copy(state_ref.at[span], held.at[span], done.at[part]))
    for copy in copies:
        copy.start()
    copies[0].wait()
    first, later, next_section = trig(angles, 0, 0), trig(angles, 0, 1), trig(angles, 1, 0)
    gates = section_gates(angles, 0)
    edge = edge_tile()
    sign1 = chunk_sign(lambda b4, b7: edge)
    for copy in copies[1:]:
        copy.wait()
    chunks, signs0 = [], []
    for c in range(CHUNKS):
        factors = [
            jnp.broadcast_to(ry(first(5), c >> 1, k >> 1) * ry(first(6), c & 1, k & 1), TILE) for k in range(CHUNKS)
        ]
        factors = [jnp.concatenate([f, f], axis=0)[None] for f in factors]
        chunks.append(to_chunk([weighted(factors, [held[halves(b0), k] for k in range(CHUNKS)]) for b0 in (0, 1)]))
        signs0.append(chunk_sign(lambda b4, b7: -edge if outer_parity(b4, c >> 1, c & 1, b7) else edge))
    chunks = chunk_layers(chunks, gates, signs0, sign1)
    for c, chunk in enumerate(chunks):
        for b0 in (0, 1):
            mixed[c, halves(b0)] = of_chunk(chunk, b0)
    later5, later6, next5, next6 = later(5), later(6), next_section(5), next_section(6)
    before = [[ry(later5, k >> 1, i >> 1) * ry(later6, k & 1, i & 1) for i in range(CHUNKS)] for k in range(CHUNKS)]
    after = [[ry(next5, o >> 1, k >> 1) * ry(next6, o & 1, k & 1) for k in range(CHUNKS)] for o in range(CHUNKS)]
    factors = {}
    for b4 in (0, 1):
        for b7 in (0, 1):
            for o in range(CHUNKS):
                for i in range(CHUNKS):
                    total = None
                    for k in range(CHUNKS):
                        term = after[o][k] * before[k][i]
                        if outer_parity(b4, k >> 1, k & 1, b7):
                            term = -term
                        total = term if total is None else total + term
                    factors[b4, b7, o, i] = jnp.broadcast_to(total, TILE)
    copies = []
    for part in range(PARTS):
        start = part * BLOCKS // PARTS
        for b4 in (0, 1):
            for b7 in (0, 1):
                rows = slice(b7 * 8, b7 * 8 + 8)
                for block in range(start + b4, start + BLOCKS // PARTS, 2):
                    tiles = [mixed[i, block, rows] for i in range(CHUNKS)]
                    for o in range(CHUNKS):
                        mixed[o, block, rows] = weighted([factors[b4, b7, o, i] for i in range(CHUNKS)], tiles)
        span = pl.ds(start, BLOCKS // PARTS)
        copies.append(pltpu.make_async_copy(mixed.at[:, span], out_ref.at[:, span], done.at[part]))
        copies[-1].start()
    for copy in copies:
        copy.wait()


def prepare_kernel(angles_ref, global_ref, gates_ref, spin_ref, sign_ref, last_ref):
    for at, (high, low) in enumerate(section_gates(angles_ref, 1)):
        gates_ref[at, 0] = high
        gates_ref[at, 1] = low
    place5, place6 = lax.axis_index("h3"), lax.axis_index("h0")
    half = global_ref[...] * 0.5
    cosines, sines = jnp.cos(half), jnp.sin(half)
    low, high = ((cosines[:, i : i + 1], sines[:, i : i + 1]) for i in (0, 1))
    later = trig(angles_ref, 1, 1)
    for o in range(CHUNKS):
        for k in range(CHUNKS):
            spin_ref[o, k] = jnp.broadcast_to(ry(high, o >> 1, k >> 1) * ry(low, o & 1, k & 1), TILE)
            last_ref[o, k] = jnp.broadcast_to(ry(later(5), o >> 1, k >> 1) * ry(later(6), o & 1, k & 1), TILE)
    edge = edge_tile()
    sign5, sign6 = signs_of(place5), signs_of(place6)
    both = signs_of(place5 * place6)
    for b4 in (0, 1):
        for b7 in (0, 1):
            factor = both
            if b4:
                factor = factor * sign5
            if b7:
                factor = factor * sign6
            sign_ref[b4, b7] = edge * factor


def middle_kernel(gates_ref, spin_ref, sign_ref, in_ref, out_ref):
    gates = [(gates_ref[at, 0], gates_ref[at, 1]) for at in range(4)]
    chunks = []
    for c in range(CHUNKS):
        factors = [jnp.concatenate([spin_ref[c, k]] * 2, axis=0)[None] for k in range(CHUNKS)]
        chunks.append(to_chunk([weighted(factors, [in_ref[k, halves(b0)] for k in range(CHUNKS)]) for b0 in (0, 1)]))
    edge = edge_tile()
    sign0 = chunk_sign(lambda b4, b7: sign_ref[b4, b7])
    chunks = chunk_layers(chunks, gates, [sign0] * CHUNKS, chunk_sign(lambda b4, b7: edge))
    for c, chunk in enumerate(chunks):
        for b0 in (0, 1):
            out_ref[c, halves(b0)] = of_chunk(chunk, b0)


def last_kernel(last_ref, in_ref, out_ref, held, done):
    factors = [[last_ref[o, k] for k in range(CHUNKS)] for o in range(CHUNKS)]
    size = BLOCKS // PARTS
    copies = []
    for part in range(PARTS):
        for block in range(part * size, part * size + size):
            for b7 in (0, 1):
                rows = slice(b7 * 8, b7 * 8 + 8)
                tiles = [in_ref[k, block, rows] for k in range(CHUNKS)]
                for o in range(CHUNKS):
                    value = weighted(factors[o], tiles)
                    held[block, o, rows] = -value if outer_parity(block & 1, o >> 1, o & 1, b7) else value
        span = pl.ds(part * size, size)
        copies.append(pltpu.make_async_copy(held.at[span], out_ref.at[span], done.at[part]))
        copies[-1].start()
    for copy in copies:
        copy.wait()


VMEM = pl.BlockSpec(memory_space=pltpu.VMEM)
HBM = pl.BlockSpec(memory_space=pltpu.HBM)
BY_CHUNK = (CHUNKS, BLOCKS, ROWS, LANES)
NATURAL = (BLOCKS, CHUNKS, ROWS, LANES)
CHUNK = (BLOCKS, ROWS, LANES)


def f32(*shape):
    return jax.ShapeDtypeStruct(shape, jnp.float32)


def call(kernel, out_shape, *args, specs=None, out_specs=VMEM, scratch=(), flops=0, limit=16):
    return pl.pallas_call(
        kernel,
        out_shape=out_shape,
        in_specs=specs or [VMEM] * len(args),
        out_specs=out_specs,
        scratch_shapes=scratch,
        cost_estimate=pl.CostEstimate(flops=flops, bytes_accessed=2 * MIB, transcendentals=0),
        compiler_params=pltpu.CompilerParams(vmem_limit_bytes=limit * MIB),
    )(*args)


def first_call(angles, state):
    return call(
        first_kernel, f32(*BY_CHUNK), angles, state, specs=[HBM, HBM], out_specs=HBM,
        scratch=[
            pltpu.VMEM(angles.shape, jnp.float32),
            pltpu.VMEM(NATURAL, jnp.float32),
            pltpu.VMEM(BY_CHUNK, jnp.float32),
            pltpu.SemaphoreType.DMA((PARTS + 1,)),
        ],
        flops=1600 * MIB, limit=62,
    )


def prepare_call(angles, global_angles):
    shapes = (
        jax.ShapeDtypeStruct((4, 2, SIDE, SIDE), jnp.bfloat16),
        f32(CHUNKS, CHUNKS, *TILE),
        f32(2, 2, *TILE),
        f32(CHUNKS, CHUNKS, *TILE),
    )
    return call(prepare_kernel, shapes, angles, global_angles, out_specs=(VMEM,) * 4, flops=400 * MIB)


def middle_call(gates, spin, sign, amps):
    return call(middle_kernel, f32(*BY_CHUNK), gates, spin, sign, amps, flops=1600 * MIB)


def last_call(last, amps):
    return call(
        last_kernel, f32(*NATURAL), last, amps, out_specs=HBM,
        scratch=[pltpu.VMEM(NATURAL, jnp.float32), pltpu.SemaphoreType.DMA((PARTS,))],
    )


def second_half(angles, global_angles, amps):
    gates, spin, sign, last = prepare_call(angles, global_angles.reshape(1, 2))
    amps = middle_call(gates, spin, sign, amps)
    amps = lax.all_to_all(
        amps.reshape(CHUNKS, BLOCKS * ROWS, LANES), ("h3", "h0"), split_axis=0, concat_axis=0, tiled=True
    )
    return last_call(last, amps.reshape(BY_CHUNK))


def on_device(state, layer_angles, global_angles):
    angles = layer_angles.transpose(0, 2, 1, 3)
    amps = first_call(angles, state.reshape(NATURAL))
    amps = lax.all_to_all(
        amps.reshape(CHUNKS * BLOCKS, ROWS, LANES), ("h3", "h0", "lo"), split_axis=0, concat_axis=0, tiled=True
    ).reshape(BY_CHUNK)
    return second_half(angles, global_angles, amps).reshape(state.shape)


def solution(mesh):
    high, low = mesh.shape["hi"], mesh.shape["lo"]
    finer = Mesh(mesh.devices.reshape(2, high // 4, 2, low), ("h3", "hm", "h0", "lo"))
    spec = P(("h3", "hm", "h0"), "lo", None)
    return jax.shard_map(on_device, mesh=finer, in_specs=(spec, P(), P()), out_specs=spec, check_vma=False)
```

time: 257 us -> 69.3 us (0.27)
  the two profiles are of different devices: /device:TPU:1 before, /device:TPU:16 now
where the time goes in v2:
time: 69.3 us; the launch traced here: 69 us
  waiting for transfers between devices  27.3 us (39%)
  blocking collectives  17.3 us (25%)
  starting transfers between devices  16 us (23%)
  Pallas kernels  7.71 us (11%)
    all_to_all x1, waiting for transfers between devices, on_device(): lax.all_to_all(amps.reshape(CHUNKS * BLOCKS, ROWS, LANES), ('h3', 'h0', '...  27.3 us
    all_to_all x1, blocking collectives, second_half(): lax.all_to_all(amps.reshape(CHUNKS, BLOCKS * ROWS, LANES), ('h3', 'h0'),...  17.3 us
    all_to_all x1, starting transfers between devices, on_device(): lax.all_to_all(amps.reshape(CHUNKS * BLOCKS, ROWS, LANES), ('h3', 'h0', '...  16 us
    pallas_call x4, Pallas kernels, call(): pl.pallas_call(kernel, out_shape=out_shape, in_specs=specs or [VMEM] * le...  7.71 us
  transfers between devices with their start and end apart: 1, of which 1 were waited for; matrix products, arithmetic and copies ran while one was open for 0% of the time, Pallas kernels for 1%

profile of v2, /device:TPU:16, one launch (start us, length us, event | category | flops | bytes accessed | tf_op | source)
XLA Modules:
  0.0 69.0 jit_solution(17004419256888521005)
XLA Ops:
  0.0 4.4 %shard_map.38 = f32[4,32,16,128]{3,2,1,0:T(8,128)} custom-call(f32[2,3,2,6]{3,2,1,0:T(2,128)} %bitcast.11, f32[32,4,16,128]{3,2,1,0:T(8,128)} %bitcast.15), custom_call_target="tpu_custom_call" | custom-call | flops 1677721600 | bytes 2097152 | tf_op jit(solution)/shard_map/pallas_call | solution.py:302
  4.4 0.0 copy-start
  4.4 16.0 %all-to-all-start = ((f32[128,16,128]{2,1,0:T(8,128)}), f32[128,16,128]{2,1,0:T(8,128)S(1)}, u32[]{:S(2)}, u32[]{:S(2)}) async-start(f32[128,16,128]{2,1,0:T(8,128)} %bitcast.14), calls=%async_computation | async-start | bytes 2097152 | tf_op jit(solution)/shard_map/all_to_all | solution.py:359
  20.4 0.0 copy-start.1
  20.4 0.0 copy-done
  20.5 0.6 copy-done.1
  21.1 0.4 shard_map.37
  21.5 27.3 %all-to-all-done = f32[128,16,128]{2,1,0:T(8,128)S(1)} async-done(((f32[128,16,128]{2,1,0:T(8,128)}), f32[128,16,128]{2,1,0:T(8,128)S(1)}, u32[]{:S(2)}, u32[]{:S(2)}) %all-to-all-start) | async-done | bytes 1048608 | tf_op jit(solution)/shard_map/all_to_all | solution.py:359
  48.8 1.9 %shard_map.39 = f32[4,32,16,128]{3,2,1,0:T(8,128)S(1)} custom-call(bf16[4,2,256,256]{3,2,1,0:T(8,128)(2,1)S(1)} %get-tuple-element.10.gates_ref, f32[4,4,8,128]{3,2,1,0:T(8,128)S(1)} %get-tuple-element.11.spin_ref, f32[2,2,8,128]{3,2,1,0:T(8,128)S(1)} %get-tuple-element.12.sign_ref, f32[4,32,16,128]{3,2,1,0:T(8,128)S(1)} %bitcast.9), custom_call_target="tpu_custom_call" | custom-call | flops 1677721600 | bytes 2097152 | tf_op jit(solution)/shard_map/pallas_call | solution.py:302
  50.7 17.3 %all_to_all.10 = f32[4,512,128]{2,1,0:T(8,128)S(1)} all-to-all(f32[4,512,128]{2,1,0:T(8,128)S(1)} %bitcast.10), channel_id=1, replica_groups=mesh['h3'=2,'hm'=4,'h0'=2,'lo'=32] {'h3','h0'}, dimensions={0} | all-to-all | bytes 2097152 | tf_op jit(solution)/shard_map/all_to_all | solution.py:350
  67.9 1.1 %shard_map.40 = f32[32,4,16,128]{3,2,1,0:T(8,128)} custom-call(f32[4,4,8,128]{3,2,1,0:T(8,128)S(1)} %get-tuple-element.9.last_ref, f32[4,32,16,128]{3,2,1,0:T(8,128)S(1)} %bitcast.8), custom_call_target="tpu_custom_call" | custom-call | bytes 2097152 | tf_op jit(solution)/shard_map/pallas_call | solution.py:302
Async XLA Ops:
  4.4 16.1 %copy-start = (f32[2,2,3,6]{3,1,2,0:T(2,128)S(1)}, f32[2,2,3,6]{3,1,2,0:T(2,128)}, u32[]{:S(2)}) copy-start(f32[2,2,3,6]{3,1,2,0:T(2,128)} %param.4) | copy-start | bytes 868
  4.4 44.4 %all-to-all-start = ((f32[128,16,128]{2,1,0:T(8,128)}), f32[128,16,128]{2,1,0:T(8,128)S(1)}, u32[]{:S(2)}, u32[]{:S(2)}) async-start(f32[128,16,128]{2,1,0:T(8,128)} %bitcast.14), calls=%async_computation | async-start | bytes 2097152 | tf_op jit(solution)/shard_map/all_to_all | solution.py:359
  20.4 0.7 copy-start.1

commit v3 on v2

--- a/solution.py
+++ b/solution.py
@@ -16,6 +16,7 @@
 ROWS = 16
 LANES = 128
 TILE = (8, LANES)
+EVERY = [(o, i) for o in range(CHUNKS) for i in range(CHUNKS)]
 MIB = 2**20
 PARTS = 4
 
@@ -170,80 +171,43 @@
     return (b4 * b5 + b5 * b6 + b6 * b7) % 2
 
 
-def first_kernel(angles_ref, state_ref, out_ref, angles, held, mixed, done):
-    copies = [pltpu.make_async_copy(angles_ref, angles, done.at[PARTS])]
-    for part in range(PARTS):
-        span = pl.ds(part * BLOCKS // PARTS, BLOCKS // PARTS)
-        copies.append(pltpu.make_async_copy(state_ref.at[span], held.at[span], done.at[part]))
-    for copy in copies:
-        copy.start()
-    copies[0].wait()
-    first, later, next_section = trig(angles, 0, 0), trig(angles, 0, 1), trig(angles, 1, 0)
-    gates = section_gates(angles, 0)
-    edge = edge_tile()
-    sign1 = chunk_sign(lambda b4, b7: edge)
-    for copy in copies[1:]:
-        copy.wait()
-    chunks, signs0 = [], []
-    for c in range(CHUNKS):
-        factors = [
-            jnp.broadcast_to(ry(first(5), c >> 1, k >> 1) * ry(first(6), c & 1, k & 1), TILE) for k in range(CHUNKS)
-        ]
-        factors = [jnp.concatenate([f, f], axis=0)[None] for f in factors]
-        chunks.append(to_chunk([weighted(factors, [held[halves(b0), k] for k in range(CHUNKS)]) for b0 in (0, 1)]))
-        signs0.append(chunk_sign(lambda b4, b7: -edge if outer_parity(b4, c >> 1, c & 1, b7) else edge))
-    chunks = chunk_layers(chunks, gates, signs0, sign1)
-    for c, chunk in enumerate(chunks):
-        for b0 in (0, 1):
-            mixed[c, halves(b0)] = of_chunk(chunk, b0)
-    later5, later6, next5, next6 = later(5), later(6), next_section(5), next_section(6)
-    before = [[ry(later5, k >> 1, i >> 1) * ry(later6, k & 1, i & 1) for i in range(CHUNKS)] for k in range(CHUNKS)]
-    after = [[ry(next5, o >> 1, k >> 1) * ry(next6, o & 1, k & 1) for k in range(CHUNKS)] for o in range(CHUNKS)]
-    factors = {}
-    for b4 in (0, 1):
-        for b7 in (0, 1):
-            for o in range(CHUNKS):
-                for i in range(CHUNKS):
-                    total = None
-                    for k in range(CHUNKS):
-                        term = after[o][k] * before[k][i]
-                        if outer_parity(b4, k >> 1, k & 1, b7):
-                            term = -term
-                        total = term if total is None else total + term
-                    factors[b4, b7, o, i] = jnp.broadcast_to(total, TILE)
-    copies = []
-    for part in range(PARTS):
-        start = part * BLOCKS // PARTS
-        for b4 in (0, 1):
-            for b7 in (0, 1):
-                rows = slice(b7 * 8, b7 * 8 + 8)
-                for block in range(start + b4, start + BLOCKS // PARTS, 2):
-                    tiles = [mixed[i, block, rows] for i in range(CHUNKS)]
-                    for o in range(CHUNKS):
-                        mixed[o, block, rows] = weighted([factors[b4, b7, o, i] for i in range(CHUNKS)], tiles)
-        span = pl.ds(start, BLOCKS // PARTS)
-        copies.append(pltpu.make_async_copy(mixed.at[:, span], out_ref.at[:, span], done.at[part]))
-        copies[-1].start()
-    for copy in copies:
-        copy.wait()
-
-
-def prepare_kernel(angles_ref, global_ref, gates_ref, spin_ref, sign_ref, last_ref):
+def pair_of(first, second, out, inner):
+    return ry(first, out >> 1, inner >> 1) * ry(second, out & 1, inner & 1)
+
+
+def prepare_first(angles_ref):
+    gates = section_gates(angles_ref, 0)
+    angles = [trig(angles_ref, *at) for at in ((0, 0), (0, 1), (1, 0))]
+    fives, sixes = [of(5) for of in angles], [of(6) for of in angles]
+    enter = [[pair_of(fives[0], sixes[0], o, i) for i in range(CHUNKS)] for o in range(CHUNKS)]
+    before = {(o, i): pair_of(fives[1], sixes[1], o, i) for o, i in EVERY}
+    after = {(o, i): pair_of(fives[2], sixes[2], o, i) for o, i in EVERY}
+    leave = {(b4, b7): [[None] * CHUNKS for _ in range(CHUNKS)] for b4 in (0, 1) for b7 in (0, 1)}
+    for o, i in EVERY:
+        terms = [after[o, k] * before[k, i] for k in range(CHUNKS)]
+        for (b4, b7), table in leave.items():
+            total = None
+            for k, term in enumerate(terms):
+                term = -term if outer_parity(b4, k >> 1, k & 1, b7) else term
+                total = term if total is None else total + term
+            table[o][i] = jnp.broadcast_to(total, TILE)
+    return gates, enter, leave
+
+
+def prepare_next(angles_ref, global_ref, gates_ref, spin_ref, sign_ref, last_ref):
     for at, (high, low) in enumerate(section_gates(angles_ref, 1)):
         gates_ref[at, 0] = high
         gates_ref[at, 1] = low
-    place5, place6 = lax.axis_index("h3"), lax.axis_index("h0")
+    later = trig(angles_ref, 1, 1)
     half = global_ref[...] * 0.5
     cosines, sines = jnp.cos(half), jnp.sin(half)
     low, high = ((cosines[:, i : i + 1], sines[:, i : i + 1]) for i in (0, 1))
-    later = trig(angles_ref, 1, 1)
-    for o in range(CHUNKS):
-        for k in range(CHUNKS):
-            spin_ref[o, k] = jnp.broadcast_to(ry(high, o >> 1, k >> 1) * ry(low, o & 1, k & 1), TILE)
-            last_ref[o, k] = jnp.broadcast_to(ry(later(5), o >> 1, k >> 1) * ry(later(6), o & 1, k & 1), TILE)
+    for o, i in EVERY:
+        spin_ref[o, i] = jnp.broadcast_to(pair_of(high, low, o, i), TILE)
+        last_ref[o, i] = jnp.broadcast_to(pair_of(later(5), later(6), o, i), TILE)
     edge = edge_tile()
-    sign5, sign6 = signs_of(place5), signs_of(place6)
-    both = signs_of(place5 * place6)
+    place5, place6 = lax.axis_index("h3"), lax.axis_index("h0")
+    sign5, sign6, both = signs_of(place5), signs_of(place6), signs_of(place5 * place6)
     for b4 in (0, 1):
         for b7 in (0, 1):
             factor = both
@@ -254,15 +218,50 @@
             sign_ref[b4, b7] = edge * factor
 
 
+def gates_of(gates_ref):
+    return [(gates_ref[at, 0], gates_ref[at, 1]) for at in range(4)]
+
+
+def mixed_chunk(factors, pieces):
+    return to_chunk([weighted(factors, [pieces(k, half) for k in range(CHUNKS)]) for half in (0, 1)])
+
+
+def first_kernel(angles_ref, global_ref, state_ref, out_ref, *refs):
+    *next_refs, angles, spins, held, done = refs
+    copies = [
+        pltpu.make_async_copy(source, target, done.at[at])
+        for at, (source, target) in enumerate([(angles_ref, angles), (global_ref, spins), (state_ref, held)])
+    ]
+    for copy in copies:
+        copy.start()
+    copies[0].wait()
+    gates, enter, leave = prepare_first(angles)
+    edge = edge_tile()
+    copies[1].wait()
+    prepare_next(angles, spins, *next_refs)
+    copies[2].wait()
+    chunks, signs0 = [], []
+    for c in range(CHUNKS):
+        chunks.append(mixed_chunk(enter[c], lambda k, half: held[halves(half), k]))
+        signs0.append(chunk_sign(lambda b4, b7: -edge if outer_parity(b4, c >> 1, c & 1, b7) else edge))
+    chunks = chunk_layers(chunks, gates, signs0, chunk_sign(lambda b4, b7: edge))
+    for c, chunk in enumerate(chunks):
+        for b0 in (0, 1):
+            out_ref[c, halves(b0)] = of_chunk(chunk, b0)
+    for (b4, b7), factors in leave.items():
+        rows = slice(b7 * 8, b7 * 8 + 8)
+        for block in range(b4, BLOCKS, 2):
+            tiles = [out_ref[i, block, rows] for i in range(CHUNKS)]
+            for o in range(CHUNKS):
+                out_ref[o, block, rows] = weighted(factors[o], tiles)
+
+
 def middle_kernel(gates_ref, spin_ref, sign_ref, in_ref, out_ref):
-    gates = [(gates_ref[at, 0], gates_ref[at, 1]) for at in range(4)]
-    chunks = []
-    for c in range(CHUNKS):
-        factors = [jnp.concatenate([spin_ref[c, k]] * 2, axis=0)[None] for k in range(CHUNKS)]
-        chunks.append(to_chunk([weighted(factors, [in_ref[k, halves(b0)] for k in range(CHUNKS)]) for b0 in (0, 1)]))
+    factors = [[jnp.concatenate([spin_ref[o, i]] * 2, axis=0)[None] for i in range(CHUNKS)] for o in range(CHUNKS)]
+    chunks = [mixed_chunk(factors[c], lambda k, half: in_ref[k, halves(half)]) for c in range(CHUNKS)]
     edge = edge_tile()
     sign0 = chunk_sign(lambda b4, b7: sign_ref[b4, b7])
-    chunks = chunk_layers(chunks, gates, [sign0] * CHUNKS, chunk_sign(lambda b4, b7: edge))
+    chunks = chunk_layers(chunks, gates_of(gates_ref), [sign0] * CHUNKS, chunk_sign(lambda b4, b7: edge))
     for c, chunk in enumerate(chunks):
         for b0 in (0, 1):
             out_ref[c, halves(b0)] = of_chunk(chunk, b0)
@@ -310,31 +309,23 @@
     )(*args)
 
 
-def first_call(angles, state):
+GATES = jax.ShapeDtypeStruct((4, 2, SIDE, SIDE), jnp.bfloat16)
+TABLE = f32(CHUNKS, CHUNKS, *TILE)
+
+
+def first_call(angles, global_angles, state):
+    shapes = (f32(*BY_CHUNK), GATES, TABLE, f32(2, 2, *TILE), TABLE)
+    args = [pltpu.with_memory_space_constraint(x, pltpu.HBM) for x in (angles, global_angles, state)]
     return call(
-        first_kernel, f32(*BY_CHUNK), angles, state, specs=[HBM, HBM], out_specs=HBM,
+        first_kernel, tuple(pltpu.VMEM(x.shape, x.dtype) for x in shapes), *args, specs=[HBM] * 3, out_specs=(VMEM,) * 5,
         scratch=[
             pltpu.VMEM(angles.shape, jnp.float32),
-            pltpu.VMEM(NATURAL, jnp.float32),
-            pltpu.VMEM(BY_CHUNK, jnp.float32),
-            pltpu.SemaphoreType.DMA((PARTS + 1,)),
+            pltpu.VMEM(global_angles.shape, jnp.float32),
+            pltpu.VMEM(state.shape, jnp.float32),
+            pltpu.SemaphoreType.DMA((3,)),
         ],
-        flops=1600 * MIB, limit=62,
-    )
-
-
-def prepare_call(angles, global_angles):
-    shapes = (
-        jax.ShapeDtypeStruct((4, 2, SIDE, SIDE), jnp.bfloat16),
-        f32(CHUNKS, CHUNKS, *TILE),
-        f32(2, 2, *TILE),
-        f32(CHUNKS, CHUNKS, *TILE),
-    )
-    return call(prepare_kernel, shapes, angles, global_angles, out_specs=(VMEM,) * 4, flops=400 * MIB)
-
-
-def middle_call(gates, spin, sign, amps):
-    return call(middle_kernel, f32(*BY_CHUNK), gates, spin, sign, amps, flops=1600 * MIB)
+        flops=1600 * MIB,
+    )
 
 
 def last_call(last, amps):
@@ -344,22 +335,18 @@
     )
 
 
-def second_half(angles, global_angles, amps):
-    gates, spin, sign, last = prepare_call(angles, global_angles.reshape(1, 2))
-    amps = middle_call(gates, spin, sign, amps)
+def on_device(state, layer_angles, global_angles):
+    amps, gates, spin, sign, last = first_call(
+        layer_angles.transpose(0, 2, 1, 3), global_angles.reshape(1, 2), state.reshape(NATURAL)
+    )
+    amps = lax.all_to_all(
+        amps.reshape(CHUNKS * BLOCKS, ROWS, LANES), ("h3", "h0", "lo"), split_axis=0, concat_axis=0, tiled=True
+    )
+    amps = call(middle_kernel, f32(*BY_CHUNK), gates, spin, sign, amps.reshape(BY_CHUNK), flops=1600 * MIB)
     amps = lax.all_to_all(
         amps.reshape(CHUNKS, BLOCKS * ROWS, LANES), ("h3", "h0"), split_axis=0, concat_axis=0, tiled=True
     )
-    return last_call(last, amps.reshape(BY_CHUNK))
-
-
-def on_device(state, layer_angles, global_angles):
-    angles = layer_angles.transpose(0, 2, 1, 3)
-    amps = first_call(angles, state.reshape(NATURAL))
-    amps = lax.all_to_all(
-        amps.reshape(CHUNKS * BLOCKS, ROWS, LANES), ("h3", "h0", "lo"), split_axis=0, concat_axis=0, tiled=True
-    ).reshape(BY_CHUNK)
-    return second_half(angles, global_angles, amps).reshape(state.shape)
+    return last_call(last, amps.reshape(BY_CHUNK)).reshape(state.shape)
 
 
 def solution(mesh):

time: 69.3 us -> 68.4 us (0.987)
  blocking collectives: 17.3 us -> 61.4 us
  waiting for transfers between devices: 27.3 us -> 0 us
  starting transfers between devices: 16 us -> 0 us
  Pallas kernels: 7.71 us -> 6.7 us
    all_to_all x1 -> x2, blocking collectives: 17.3 us -> 61.4 us  [the longest x1 44.2 us: on_device(): lax.all_to_all(amps.reshape(CHUNKS * BLOCKS, ROWS, LANES), ('h3', 'h0', '...]
    all_to_all x1 -> x0, waiting for transfers between devices: 27.3 us -> none  [on_device(): lax.all_to_all(amps.reshape(CHUNKS * BLOCKS, ROWS, LANES), ('h3', 'h0', '...]
    all_to_all x1 -> x0, starting transfers between devices: 16 us -> none  [on_device(): lax.all_to_all(amps.reshape(CHUNKS * BLOCKS, ROWS, LANES), ('h3', 'h0', '...]
    pallas_call x4 -> x3, Pallas kernels: 7.71 us -> 6.7 us  [call(): pl.pallas_call(kernel, out_shape=out_shape, in_specs=specs or [VMEM] * le...]
  transfers between devices with their start and end apart: 1 -> 0, of which waited for: 1 -> 0; matrix products, arithmetic and copies ran while one was open for 0% -> 0% of each run, Pallas kernels for 1% -> 0%
where the time goes in v3:
time: 68.4 us; the launch traced here: 68.2 us
  blocking collectives  61.4 us (90%)
  Pallas kernels  6.7 us (10%)
    all_to_all x1, blocking collectives, on_device(): lax.all_to_all(amps.reshape(CHUNKS * BLOCKS, ROWS, LANES), ('h3', 'h0', '...  44.2 us
    all_to_all x1, blocking collectives, on_device(): lax.all_to_all(amps.reshape(CHUNKS, BLOCKS * ROWS, LANES), ('h3', 'h0'),...  17.3 us
    pallas_call x3, Pallas kernels, call(): pl.pallas_call(kernel, out_shape=out_shape, in_specs=specs or [VMEM] * le...  6.7 us

profile of v3, /device:TPU:16, one launch (start us, length us, event | category | flops | bytes accessed | tf_op | source)
XLA Modules:
  0.0 68.2 jit_solution(16490199030275823125)
XLA Ops:
  0.0 3.8 %shard_map.37 = (f32[4,32,16,128]{3,2,1,0:T(8,128)S(1)}, bf16[4,2,256,256]{3,2,1,0:T(8,128)(2,1)S(1)}, f32[4,4,8,128]{3,2,1,0:T(8,128)S(1)}, f32[2,2,8,128]{3,2,1,0:T(8,128)S(1)}, f32[4,4,8,128]{3,2,1,0:T(8,128)S(1)}) custom-call(f32[2,3,2,6]{3,2,1,0:T(2,128)} %bitcast.13, f32[1,2]{1,0:T(1,128)} %bitcast.14, f32[32,4,16,128]{3,2,1,0:T(8,128)} %bitcast.12), custom_call_target="tpu_custom_call" | custom-call | flops 1677721600 | bytes 2097152 | tf_op jit(solution)/shard_map/pallas_call | solution.py:301
  3.8 44.2 %all_to_all.10 = f32[128,16,128]{2,1,0:T(8,128)S(1)} all-to-all(f32[128,16,128]{2,1,0:T(8,128)S(1)} %bitcast.9), channel_id=1, replica_groups=mesh['h3'=2,'hm'=4,'h0'=2,'lo'=32] {'h3','h0','lo'}, dimensions={0} | all-to-all | bytes 2097152 | tf_op jit(solution)/shard_map/all_to_all | solution.py:342
  48.0 1.9 %shard_map.38 = f32[4,32,16,128]{3,2,1,0:T(8,128)S(1)} custom-call(bf16[4,2,256,256]{3,2,1,0:T(8,128)(2,1)S(1)} %get-tuple-element.11.gates_ref, f32[4,4,8,128]{3,2,1,0:T(8,128)S(1)} %get-tuple-element.12.spin_ref, f32[2,2,8,128]{3,2,1,0:T(8,128)S(1)} %get-tuple-element.13.sign_ref, f32[4,32,16,128]{3,2,1,0:T(8,128)S(1)} %bitcast.10), custom_call_target="tpu_custom_call" | custom-call | flops 1677721600 | bytes 2097152 | tf_op jit(solution)/shard_map/pallas_call | solution.py:301
  49.8 17.3 %all_to_all.11 = f32[4,512,128]{2,1,0:T(8,128)S(1)} all-to-all(f32[4,512,128]{2,1,0:T(8,128)S(1)} %bitcast.11), channel_id=1, replica_groups=mesh['h3'=2,'hm'=4,'h0'=2,'lo'=32] {'h3','h0'}, dimensions={0} | all-to-all | bytes 2097152 | tf_op jit(solution)/shard_map/all_to_all | solution.py:346
  67.1 1.1 %shard_map.39 = f32[32,4,16,128]{3,2,1,0:T(8,128)} custom-call(f32[4,4,8,128]{3,2,1,0:T(8,128)S(1)} %get-tuple-element.10.last_ref, f32[4,32,16,128]{3,2,1,0:T(8,128)S(1)} %bitcast.8), custom_call_target="tpu_custom_call" | custom-call | bytes 2097152 | tf_op jit(solution)/shard_map/pallas_call | solution.py:301

commit v4 on v3

--- a/solution.py
+++ b/solution.py
@@ -167,6 +167,10 @@
     return slice(half * 16, half * 16 + 16)
 
 
+def rows_of(b7):
+    return slice(b7 * 8, b7 * 8 + 8)
+
+
 def outer_parity(b4, b5, b6, b7):
     return (b4 * b5 + b5 * b6 + b6 * b7) % 2
 
@@ -243,47 +247,87 @@
     chunks, signs0 = [], []
     for c in range(CHUNKS):
         chunks.append(mixed_chunk(enter[c], lambda k, half: held[halves(half), k]))
-        signs0.append(chunk_sign(lambda b4, b7: -edge if outer_parity(b4, c >> 1, c & 1, b7) else edge))
+        signs0.append(outer_signs(edge, c))
     chunks = chunk_layers(chunks, gates, signs0, chunk_sign(lambda b4, b7: edge))
     for c, chunk in enumerate(chunks):
         for b0 in (0, 1):
             out_ref[c, halves(b0)] = of_chunk(chunk, b0)
     for (b4, b7), factors in leave.items():
-        rows = slice(b7 * 8, b7 * 8 + 8)
         for block in range(b4, BLOCKS, 2):
-            tiles = [out_ref[i, block, rows] for i in range(CHUNKS)]
+            tiles = [out_ref[i, block, rows_of(b7)] for i in range(CHUNKS)]
             for o in range(CHUNKS):
-                out_ref[o, block, rows] = weighted(factors[o], tiles)
+                out_ref[o, block, rows_of(b7)] = weighted(factors[o], tiles)
+
+
+def late():
+    return lax.rem(lax.axis_index("lo"), 2) == 1
+
+
+def outer_signs(edge, c):
+    return chunk_sign(lambda b4, b7: -edge if outer_parity(b4, c >> 1, c & 1, b7) else edge)
 
 
 def middle_kernel(gates_ref, spin_ref, sign_ref, in_ref, out_ref):
-    factors = [[jnp.concatenate([spin_ref[o, i]] * 2, axis=0)[None] for i in range(CHUNKS)] for o in range(CHUNKS)]
-    chunks = [mixed_chunk(factors[c], lambda k, half: in_ref[k, halves(half)]) for c in range(CHUNKS)]
-    edge = edge_tile()
-    sign0 = chunk_sign(lambda b4, b7: sign_ref[b4, b7])
-    chunks = chunk_layers(chunks, gates_of(gates_ref), [sign0] * CHUNKS, chunk_sign(lambda b4, b7: edge))
-    for c, chunk in enumerate(chunks):
-        for b0 in (0, 1):
-            out_ref[c, halves(b0)] = of_chunk(chunk, b0)
-
-
-def last_kernel(last_ref, in_ref, out_ref, held, done):
-    factors = [[last_ref[o, k] for k in range(CHUNKS)] for o in range(CHUNKS)]
-    size = BLOCKS // PARTS
-    copies = []
-    for part in range(PARTS):
-        for block in range(part * size, part * size + size):
+    @pl.when(late())
+    def _():
+        factors = [[spin_ref[o, i] for i in range(CHUNKS)] for o in range(CHUNKS)]
+        for block in range(BLOCKS):
             for b7 in (0, 1):
-                rows = slice(b7 * 8, b7 * 8 + 8)
-                tiles = [in_ref[k, block, rows] for k in range(CHUNKS)]
+                tiles = [in_ref[i, block, rows_of(b7)] for i in range(CHUNKS)]
                 for o in range(CHUNKS):
-                    value = weighted(factors[o], tiles)
-                    held[block, o, rows] = -value if outer_parity(block & 1, o >> 1, o & 1, b7) else value
-        span = pl.ds(part * size, size)
-        copies.append(pltpu.make_async_copy(held.at[span], out_ref.at[span], done.at[part]))
-        copies[-1].start()
-    for copy in copies:
-        copy.wait()
+                    out_ref[o, block, rows_of(b7)] = weighted(factors[o], tiles)
+
+    @pl.when(jnp.logical_not(late()))
+    def _():
+        factors = [[jnp.concatenate([spin_ref[o, i]] * 2, axis=0)[None] for i in range(CHUNKS)] for o in range(CHUNKS)]
+        chunks = [mixed_chunk(factors[c], lambda k, half: in_ref[k, halves(half)]) for c in range(CHUNKS)]
+        edge = edge_tile()
+        sign0 = chunk_sign(lambda b4, b7: sign_ref[b4, b7])
+        chunks = chunk_layers(chunks, gates_of(gates_ref), [sign0] * CHUNKS, chunk_sign(lambda b4, b7: edge))
+        for c, chunk in enumerate(chunks):
+            for b0 in (0, 1):
+                out_ref[c, halves(b0)] = of_chunk(chunk, b0)
+
+
+def last_kernel(gates_ref, last_ref, in_ref, out_ref, held, done):
+    @pl.when(late())
+    def _():
+        right0, left0, right1, left1 = gates_of(gates_ref)
+        edge = edge_tile()
+        chunks = [to_chunk([in_ref[c, halves(b0)] for b0 in (0, 1)]) for c in range(CHUNKS)]
+        chunks = [dot3(split(chunk), right0) for chunk in chunks]
+        chunks = [dot3(left0, split(chunk)) * outer_signs(edge, c) for c, chunk in enumerate(chunks)]
+        factors = [[last_ref[o, i][0:1, 0:1] for i in range(CHUNKS)] for o in range(CHUNKS)]
+        chunks = [weighted(factors[o], chunks) for o in range(CHUNKS)]
+        chunks = [dot3(split(chunk), right1) for chunk in chunks]
+        copies = []
+        for c, chunk in enumerate(chunks):
+            chunk = dot3(left1, split(chunk)) * outer_signs(edge, c)
+            for b0 in (0, 1):
+                held[halves(b0), c] = of_chunk(chunk, b0)
+            copies.append(pltpu.make_async_copy(held.at[:, c], out_ref.at[:, c], done.at[c]))
+            copies[-1].start()
+        for copy in copies:
+            copy.wait()
+
+    @pl.when(jnp.logical_not(late()))
+    def _():
+        factors = [[last_ref[o, i] for i in range(CHUNKS)] for o in range(CHUNKS)]
+        size = BLOCKS // PARTS
+        copies = []
+        for part in range(PARTS):
+            for block in range(part * size, part * size + size):
+                for b7 in (0, 1):
+                    tiles = [in_ref[i, block, rows_of(b7)] for i in range(CHUNKS)]
+                    for o in range(CHUNKS):
+                        value = weighted(factors[o], tiles)
+                        value = -value if outer_parity(block & 1, o >> 1, o & 1, b7) else value
+                        held[block, o, rows_of(b7)] = value
+            span = pl.ds(part * size, size)
+            copies.append(pltpu.make_async_copy(held.at[span], out_ref.at[span], done.at[part]))
+            copies[-1].start()
+        for copy in copies:
+            copy.wait()
 
 
 VMEM = pl.BlockSpec(memory_space=pltpu.VMEM)
@@ -328,9 +372,9 @@
     )
 
 
-def last_call(last, amps):
+def last_call(gates, last, amps):
     return call(
-        last_kernel, f32(*NATURAL), last, amps, out_specs=HBM,
+        last_kernel, f32(*NATURAL), gates, last, amps, out_specs=HBM,
         scratch=[pltpu.VMEM(NATURAL, jnp.float32), pltpu.SemaphoreType.DMA((PARTS,))],
     )
 
@@ -346,7 +390,7 @@
     amps = lax.all_to_all(
         amps.reshape(CHUNKS, BLOCKS * ROWS, LANES), ("h3", "h0"), split_axis=0, concat_axis=0, tiled=True
     )
-    return last_call(last, amps.reshape(BY_CHUNK)).reshape(state.shape)
+    return last_call(gates, last, amps.reshape(BY_CHUNK)).reshape(state.shape)
 
 
 def solution(mesh):

time: 68.4 us -> 66.7 us (0.975)
  blocking collectives: 61.4 us -> 59.8 us
    all_to_all x1, blocking collectives: 17.3 us -> 15.6 us  [on_device(): lax.all_to_all(amps.reshape(CHUNKS, BLOCKS * ROWS, LANES), ('h3', 'h0'),...]
where the time goes in v4:
time: 66.7 us; the launch traced here: 66.5 us
  blocking collectives  59.8 us (90%)
  Pallas kernels  6.7 us (10%)
    all_to_all x1, blocking collectives, on_device(): lax.all_to_all(amps.reshape(CHUNKS * BLOCKS, ROWS, LANES), ('h3', 'h0', '...  44.2 us
    all_to_all x1, blocking collectives, on_device(): lax.all_to_all(amps.reshape(CHUNKS, BLOCKS * ROWS, LANES), ('h3', 'h0'),...  15.6 us
    pallas_call x3, Pallas kernels, call(): pl.pallas_call(kernel, out_shape=out_shape, in_specs=specs or [VMEM] * le...  6.7 us

profile of v4, /device:TPU:16, one launch (start us, length us, event | category | flops | bytes accessed | tf_op | source)
XLA Modules:
  0.0 66.5 jit_solution(4639107229258433013)
XLA Ops:
  0.0 3.8 %shard_map.37 = (f32[4,32,16,128]{3,2,1,0:T(8,128)S(1)}, bf16[4,2,256,256]{3,2,1,0:T(8,128)(2,1)S(1)}, f32[4,4,8,128]{3,2,1,0:T(8,128)S(1)}, f32[2,2,8,128]{3,2,1,0:T(8,128)S(1)}, f32[4,4,8,128]{3,2,1,0:T(8,128)S(1)}) custom-call(f32[2,3,2,6]{3,2,1,0:T(2,128)} %bitcast.13, f32[1,2]{1,0:T(1,128)} %bitcast.14, f32[32,4,16,128]{3,2,1,0:T(8,128)} %bitcast.12), custom_call_target="tpu_custom_call" | custom-call | flops 1677721600 | bytes 2097152 | tf_op jit(solution)/shard_map/pallas_call | solution.py:345
  3.8 44.2 %all_to_all.10 = f32[128,16,128]{2,1,0:T(8,128)S(1)} all-to-all(f32[128,16,128]{2,1,0:T(8,128)S(1)} %bitcast.9), channel_id=1, replica_groups=mesh['h3'=2,'hm'=4,'h0'=2,'lo'=32] {'h3','h0','lo'}, dimensions={0} | all-to-all | bytes 2097152 | tf_op jit(solution)/shard_map/all_to_all | solution.py:386
  48.0 1.9 %shard_map.38 = f32[4,32,16,128]{3,2,1,0:T(8,128)S(1)} custom-call(bf16[4,2,256,256]{3,2,1,0:T(8,128)(2,1)S(1)} %get-tuple-element.10.gates_ref, f32[4,4,8,128]{3,2,1,0:T(8,128)S(1)} %get-tuple-element.12.spin_ref, f32[2,2,8,128]{3,2,1,0:T(8,128)S(1)} %get-tuple-element.13.sign_ref, f32[4,32,16,128]{3,2,1,0:T(8,128)S(1)} %bitcast.10), custom_call_target="tpu_custom_call" | custom-call | flops 1677721600 | bytes 2097152 | tf_op jit(solution)/shard_map/pallas_call | solution.py:345
  49.8 15.6 %all_to_all.11 = f32[4,512,128]{2,1,0:T(8,128)S(1)} all-to-all(f32[4,512,128]{2,1,0:T(8,128)S(1)} %bitcast.11), channel_id=1, replica_groups=mesh['h3'=2,'hm'=4,'h0'=2,'lo'=32] {'h3','h0'}, dimensions={0} | all-to-all | bytes 2097152 | tf_op jit(solution)/shard_map/all_to_all | solution.py:390
  65.5 1.1 %shard_map.39 = f32[32,4,16,128]{3,2,1,0:T(8,128)} custom-call(bf16[4,2,256,256]{3,2,1,0:T(8,128)(2,1)S(1)} %get-tuple-element.10.gates_ref, f32[4,4,8,128]{3,2,1,0:T(8,128)S(1)} %get-tuple-element.11.last_ref, f32[4,32,16,128]{3,2,1,0:T(8,128)S(1)} %bitcast.8), custom_call_target="tpu_custom_call" | custom-call | bytes 2097152 | tf_op jit(solution)/shard_map/pallas_call | solution.py:345

commit v5 on v4

--- a/solution.py
+++ b/solution.py
@@ -167,6 +167,11 @@
     return slice(half * 16, half * 16 + 16)
 
 
+def spot(c, block):
+    z, x, core = block // 8, block // 2 % 4, block % 2
+    return (((c % 2) * 4 + x) * 2 + core) * 8 + (c // 2) * 4 + z
+
+
 def rows_of(b7):
     return slice(b7 * 8, b7 * 8 + 8)
 
@@ -198,10 +203,8 @@
     return gates, enter, leave
 
 
-def prepare_next(angles_ref, global_ref, gates_ref, spin_ref, sign_ref, last_ref):
-    for at, (high, low) in enumerate(section_gates(angles_ref, 1)):
-        gates_ref[at, 0] = high
-        gates_ref[at, 1] = low
+def prepare_next(angles_ref, global_ref, kept_ref, spin_ref, sign_ref, last_ref):
+    kept_ref[...] = angles_ref[...]
     later = trig(angles_ref, 1, 1)
     half = global_ref[...] * 0.5
     cosines, sines = jnp.cos(half), jnp.sin(half)
@@ -220,10 +223,6 @@
             if b7:
                 factor = factor * sign6
             sign_ref[b4, b7] = edge * factor
-
-
-def gates_of(gates_ref):
-    return [(gates_ref[at, 0], gates_ref[at, 1]) for at in range(4)]
 
 
 def mixed_chunk(factors, pieces):
@@ -251,48 +250,53 @@
     chunks = chunk_layers(chunks, gates, signs0, chunk_sign(lambda b4, b7: edge))
     for c, chunk in enumerate(chunks):
         for b0 in (0, 1):
-            out_ref[c, halves(b0)] = of_chunk(chunk, b0)
+            piece = of_chunk(chunk, b0)
+            for at in range(16):
+                out_ref[spot(c, b0 * 16 + at)] = piece[at]
     for (b4, b7), factors in leave.items():
         for block in range(b4, BLOCKS, 2):
-            tiles = [out_ref[i, block, rows_of(b7)] for i in range(CHUNKS)]
+            tiles = [out_ref[spot(i, block), rows_of(b7)] for i in range(CHUNKS)]
             for o in range(CHUNKS):
-                out_ref[o, block, rows_of(b7)] = weighted(factors[o], tiles)
+                out_ref[spot(o, block), rows_of(b7)] = weighted(factors[o], tiles)
 
 
 def late():
-    return lax.rem(lax.axis_index("lo"), 2) == 1
+    return lax.axis_index("core") == 1
 
 
 def outer_signs(edge, c):
     return chunk_sign(lambda b4, b7: -edge if outer_parity(b4, c >> 1, c & 1, b7) else edge)
 
 
-def middle_kernel(gates_ref, spin_ref, sign_ref, in_ref, out_ref):
+def middle_kernel(angles_ref, spin_ref, sign_ref, in_ref, out_ref):
     @pl.when(late())
     def _():
         factors = [[spin_ref[o, i] for i in range(CHUNKS)] for o in range(CHUNKS)]
         for block in range(BLOCKS):
             for b7 in (0, 1):
-                tiles = [in_ref[i, block, rows_of(b7)] for i in range(CHUNKS)]
+                tiles = [in_ref[spot(i, block), rows_of(b7)] for i in range(CHUNKS)]
                 for o in range(CHUNKS):
                     out_ref[o, block, rows_of(b7)] = weighted(factors[o], tiles)
 
     @pl.when(jnp.logical_not(late()))
     def _():
+        def half_of(k, half):
+            return jnp.stack([in_ref[spot(k, half * 16 + at)] for at in range(16)])
+
         factors = [[jnp.concatenate([spin_ref[o, i]] * 2, axis=0)[None] for i in range(CHUNKS)] for o in range(CHUNKS)]
-        chunks = [mixed_chunk(factors[c], lambda k, half: in_ref[k, halves(half)]) for c in range(CHUNKS)]
+        chunks = [mixed_chunk(factors[c], half_of) for c in range(CHUNKS)]
         edge = edge_tile()
         sign0 = chunk_sign(lambda b4, b7: sign_ref[b4, b7])
-        chunks = chunk_layers(chunks, gates_of(gates_ref), [sign0] * CHUNKS, chunk_sign(lambda b4, b7: edge))
+        chunks = chunk_layers(chunks, section_gates(angles_ref, 1), [sign0] * CHUNKS, chunk_sign(lambda b4, b7: edge))
         for c, chunk in enumerate(chunks):
             for b0 in (0, 1):
                 out_ref[c, halves(b0)] = of_chunk(chunk, b0)
 
 
-def last_kernel(gates_ref, last_ref, in_ref, out_ref, held, done):
+def last_kernel(angles_ref, last_ref, in_ref, out_ref, held, done):
     @pl.when(late())
     def _():
-        right0, left0, right1, left1 = gates_of(gates_ref)
+        right0, left0, right1, left1 = section_gates(angles_ref, 1)
         edge = edge_tile()
         chunks = [to_chunk([in_ref[c, halves(b0)] for b0 in (0, 1)]) for c in range(CHUNKS)]
         chunks = [dot3(split(chunk), right0) for chunk in chunks]
@@ -337,6 +341,10 @@
 CHUNK = (BLOCKS, ROWS, LANES)
 
 
+BY_SPOT = (CHUNKS * BLOCKS, ROWS, LANES)
+GROUP = ("h0", "x", "core", "h3", "z")
+
+
 def f32(*shape):
     return jax.ShapeDtypeStruct(shape, jnp.float32)
 
@@ -353,12 +361,11 @@
     )(*args)
 
 
-GATES = jax.ShapeDtypeStruct((4, 2, SIDE, SIDE), jnp.bfloat16)
 TABLE = f32(CHUNKS, CHUNKS, *TILE)
 
 
 def first_call(angles, global_angles, state):
-    shapes = (f32(*BY_CHUNK), GATES, TABLE, f32(2, 2, *TILE), TABLE)
+    shapes = (f32(*BY_SPOT), f32(*angles.shape), TABLE, f32(2, 2, *TILE), TABLE)
     args = [pltpu.with_memory_space_constraint(x, pltpu.HBM) for x in (angles, global_angles, state)]
     return call(
         first_kernel, tuple(pltpu.VMEM(x.shape, x.dtype) for x in shapes), *args, specs=[HBM] * 3, out_specs=(VMEM,) * 5,
@@ -372,29 +379,28 @@
     )
 
 
-def last_call(gates, last, amps):
+def last_call(angles, last, amps):
     return call(
-        last_kernel, f32(*NATURAL), gates, last, amps, out_specs=HBM,
+        last_kernel, f32(*NATURAL), angles, last, amps, out_specs=HBM,
         scratch=[pltpu.VMEM(NATURAL, jnp.float32), pltpu.SemaphoreType.DMA((PARTS,))],
     )
 
 
 def on_device(state, layer_angles, global_angles):
-    amps, gates, spin, sign, last = first_call(
+    amps, angles, spin, sign, last = first_call(
         layer_angles.transpose(0, 2, 1, 3), global_angles.reshape(1, 2), state.reshape(NATURAL)
     )
-    amps = lax.all_to_all(
-        amps.reshape(CHUNKS * BLOCKS, ROWS, LANES), ("h3", "h0", "lo"), split_axis=0, concat_axis=0, tiled=True
-    )
-    amps = call(middle_kernel, f32(*BY_CHUNK), gates, spin, sign, amps.reshape(BY_CHUNK), flops=1600 * MIB)
+    amps = lax.all_to_all(amps, GROUP, split_axis=0, concat_axis=0, tiled=True)
+    amps = call(middle_kernel, f32(*BY_CHUNK), angles, spin, sign, amps, flops=1600 * MIB)
     amps = lax.all_to_all(
         amps.reshape(CHUNKS, BLOCKS * ROWS, LANES), ("h3", "h0"), split_axis=0, concat_axis=0, tiled=True
     )
-    return last_call(gates, last, amps.reshape(BY_CHUNK)).reshape(state.shape)
+    return last_call(angles, last, amps.reshape(BY_CHUNK)).reshape(state.shape)
 
 
 def solution(mesh):
     high, low = mesh.shape["hi"], mesh.shape["lo"]
-    finer = Mesh(mesh.devices.reshape(2, high // 4, 2, low), ("h3", "hm", "h0", "lo"))
-    spec = P(("h3", "hm", "h0"), "lo", None)
+    sizes = (2, high // 4, 2, 4, low // 8, 2)
+    finer = Mesh(mesh.devices.reshape(sizes), ("h3", "hm", "h0", "z", "x", "core"))
+    spec = P(("h3", "hm", "h0"), ("z", "x", "core"), None)
     return jax.shard_map(on_device, mesh=finer, in_specs=(spec, P(), P()), out_specs=spec, check_vma=False)

time: 66.7 us -> 66.5 us (level)
  no operation moved by 1% of the time
where the time goes in v5:
time: 66.5 us; the launch traced here: 66.3 us
  blocking collectives  59.5 us (89%)
  Pallas kernels  6.78 us (10%)
    all_to_all x1, blocking collectives, on_device(): amps = lax.all_to_all(amps, GROUP, split_axis=0, concat_axis=0, tiled=True)  44.5 us
    all_to_all x1, blocking collectives, on_device(): lax.all_to_all(amps.reshape(CHUNKS, BLOCKS * ROWS, LANES), ('h3', 'h0'),...  15 us
    pallas_call x3, Pallas kernels, call(): pl.pallas_call(kernel, out_shape=out_shape, in_specs=specs or [VMEM] * le...  6.78 us

profile of v5, /device:TPU:16, one launch (start us, length us, event | category | flops | bytes accessed | tf_op | source)
XLA Modules:
  0.0 66.3 jit_solution(8225739738896323322)
XLA Ops:
  0.0 3.6 %shard_map.37 = (f32[128,16,128]{2,1,0:T(8,128)S(1)}, f32[2,3,2,6]{3,2,1,0:T(2,128)S(1)}, f32[4,4,8,128]{3,2,1,0:T(8,128)S(1)}, f32[2,2,8,128]{3,2,1,0:T(8,128)S(1)}, f32[4,4,8,128]{3,2,1,0:T(8,128)S(1)}) custom-call(f32[2,3,2,6]{3,2,1,0:T(2,128)} %bitcast.9, f32[1,2]{1,0:T(1,128)} %bitcast.10, f32[32,4,16,128]{3,2,1,0:T(8,128)} %bitcast.8), custom_call_target="tpu_custom_call" | custom-call | flops 1677721600 | bytes 2097152 | tf_op jit(solution)/shard_map/pallas_call | solution.py:353
  3.6 44.5 %all_to_all.10.in_ref = f32[128,16,128]{2,1,0:T(8,128)S(1)} all-to-all(f32[128,16,128]{2,1,0:T(8,128)S(1)} %get-tuple-element.14), channel_id=1, replica_groups=mesh['h3'=2,'hm'=4,'h0'=2,'z'=4,'x'=4,'core'=2] {'h0','x','core','h3','z'}, dimensions={0} | all-to-all | bytes 2097152 | tf_op jit(solution)/shard_map/all_to_all | solution.py:393
  48.1 2.2 %shard_map.38 = f32[4,32,16,128]{3,2,1,0:T(8,128)S(1)} custom-call(f32[2,3,2,6]{3,2,1,0:T(2,128)S(1)} %get-tuple-element.10.angles_ref, f32[4,4,8,128]{3,2,1,0:T(8,128)S(1)} %get-tuple-element.12.spin_ref, f32[2,2,8,128]{3,2,1,0:T(8,128)S(1)} %get-tuple-element.13.sign_ref, f32[128,16,128]{2,1,0:T(8,128)S(1)} %all_to_all.10.in_ref), custom_call_target="tpu_custom_call" | custom-call | flops 1677721600 | bytes 2097152 | tf_op jit(solution)/shard_map/pallas_call | solution.py:353
  50.2 15.0 %all_to_all.11 = f32[4,512,128]{2,1,0:T(8,128)S(1)} all-to-all(f32[4,512,128]{2,1,0:T(8,128)S(1)} %bitcast.7), channel_id=1, replica_groups=mesh['h3'=2,'hm'=4,'h0'=2,'z'=4,'x'=4,'core'=2] {'h3','h0'}, dimensions={0} | all-to-all | bytes 2097152 | tf_op jit(solution)/shard_map/all_to_all | solution.py:395
  65.3 1.1 %shard_map.39 = f32[32,4,16,128]{3,2,1,0:T(8,128)} custom-call(f32[2,3,2,6]{3,2,1,0:T(2,128)S(1)} %get-tuple-element.10.angles_ref, f32[4,4,8,128]{3,2,1,0:T(8,128)S(1)} %get-tuple-element.11.last_ref, f32[4,32,16,128]{3,2,1,0:T(8,128)S(1)} %bitcast.6), custom_call_target="tpu_custom_call" | custom-call | bytes 2097152 | tf_op jit(solution)/shard_map/pallas_call | solution.py:353

commit v6 on v5

--- a/solution.py
+++ b/solution.py
@@ -172,6 +172,10 @@
     return (((c % 2) * 4 + x) * 2 + core) * 8 + (c // 2) * 4 + z
 
 
+def seat(c):
+    return c % 2 * 2 + c // 2
+
+
 def rows_of(b7):
     return slice(b7 * 8, b7 * 8 + 8)
 
@@ -276,7 +280,7 @@
             for b7 in (0, 1):
                 tiles = [in_ref[spot(i, block), rows_of(b7)] for i in range(CHUNKS)]
                 for o in range(CHUNKS):
-                    out_ref[o, block, rows_of(b7)] = weighted(factors[o], tiles)
+                    out_ref[seat(o), block, rows_of(b7)] = weighted(factors[o], tiles)
 
     @pl.when(jnp.logical_not(late()))
     def _():
@@ -290,7 +294,7 @@
         chunks = chunk_layers(chunks, section_gates(angles_ref, 1), [sign0] * CHUNKS, chunk_sign(lambda b4, b7: edge))
         for c, chunk in enumerate(chunks):
             for b0 in (0, 1):
-                out_ref[c, halves(b0)] = of_chunk(chunk, b0)
+                out_ref[seat(c), halves(b0)] = of_chunk(chunk, b0)
 
 
 def last_kernel(angles_ref, last_ref, in_ref, out_ref, held, done):
@@ -298,7 +302,7 @@
     def _():
         right0, left0, right1, left1 = section_gates(angles_ref, 1)
         edge = edge_tile()
-        chunks = [to_chunk([in_ref[c, halves(b0)] for b0 in (0, 1)]) for c in range(CHUNKS)]
+        chunks = [to_chunk([in_ref[seat(c), halves(b0)] for b0 in (0, 1)]) for c in range(CHUNKS)]
         chunks = [dot3(split(chunk), right0) for chunk in chunks]
         chunks = [dot3(left0, split(chunk)) * outer_signs(edge, c) for c, chunk in enumerate(chunks)]
         factors = [[last_ref[o, i][0:1, 0:1] for i in range(CHUNKS)] for o in range(CHUNKS)]
@@ -322,7 +326,7 @@
         for part in range(PARTS):
             for block in range(part * size, part * size + size):
                 for b7 in (0, 1):
-                    tiles = [in_ref[i, block, rows_of(b7)] for i in range(CHUNKS)]
+                    tiles = [in_ref[seat(i), block, rows_of(b7)] for i in range(CHUNKS)]
                     for o in range(CHUNKS):
                         value = weighted(factors[o], tiles)
                         value = -value if outer_parity(block & 1, o >> 1, o & 1, b7) else value
@@ -393,7 +397,7 @@
     amps = lax.all_to_all(amps, GROUP, split_axis=0, concat_axis=0, tiled=True)
     amps = call(middle_kernel, f32(*BY_CHUNK), angles, spin, sign, amps, flops=1600 * MIB)
     amps = lax.all_to_all(
-        amps.reshape(CHUNKS, BLOCKS * ROWS, LANES), ("h3", "h0"), split_axis=0, concat_axis=0, tiled=True
+        amps.reshape(CHUNKS, BLOCKS * ROWS, LANES), ("h0", "h3"), split_axis=0, concat_axis=0, tiled=True
     )
     return last_call(angles, last, amps.reshape(BY_CHUNK)).reshape(state.shape)
 

time: 66.5 us -> 66.5 us (level)
  no operation moved by 1% of the time
where the time goes in v6:
time: 66.5 us; the launch traced here: 66.3 us
  blocking collectives  59.5 us (89%)
  Pallas kernels  6.78 us (10%)
    all_to_all x1, blocking collectives, on_device(): amps = lax.all_to_all(amps, GROUP, split_axis=0, concat_axis=0, tiled=True)  44.5 us
    all_to_all x1, blocking collectives, on_device(): lax.all_to_all(amps.reshape(CHUNKS, BLOCKS * ROWS, LANES), ('h0', 'h3'),...  15 us
    pallas_call x3, Pallas kernels, call(): pl.pallas_call(kernel, out_shape=out_shape, in_specs=specs or [VMEM] * le...  6.78 us

profile of v6, /device:TPU:16, one launch (start us, length us, event | category | flops | bytes accessed | tf_op | source)
XLA Modules:
  0.0 66.3 jit_solution(4948632466353803408)
XLA Ops:
  0.0 3.6 %shard_map.37 = (f32[128,16,128]{2,1,0:T(8,128)S(1)}, f32[2,3,2,6]{3,2,1,0:T(2,128)S(1)}, f32[4,4,8,128]{3,2,1,0:T(8,128)S(1)}, f32[2,2,8,128]{3,2,1,0:T(8,128)S(1)}, f32[4,4,8,128]{3,2,1,0:T(8,128)S(1)}) custom-call(f32[2,3,2,6]{3,2,1,0:T(2,128)} %bitcast.9, f32[1,2]{1,0:T(1,128)} %bitcast.10, f32[32,4,16,128]{3,2,1,0:T(8,128)} %bitcast.8), custom_call_target="tpu_custom_call" | custom-call | flops 1677721600 | bytes 2097152 | tf_op jit(solution)/shard_map/pallas_call | solution.py:357
  3.6 44.5 %all_to_all.10.in_ref = f32[128,16,128]{2,1,0:T(8,128)S(1)} all-to-all(f32[128,16,128]{2,1,0:T(8,128)S(1)} %get-tuple-element.14), channel_id=1, replica_groups=mesh['h3'=2,'hm'=4,'h0'=2,'z'=4,'x'=4,'core'=2] {'h0','x','core','h3','z'}, dimensions={0} | all-to-all | bytes 2097152 | tf_op jit(solution)/shard_map/all_to_all | solution.py:397
  48.1 2.2 %shard_map.38 = f32[4,32,16,128]{3,2,1,0:T(8,128)S(1)} custom-call(f32[2,3,2,6]{3,2,1,0:T(2,128)S(1)} %get-tuple-element.10.angles_ref, f32[4,4,8,128]{3,2,1,0:T(8,128)S(1)} %get-tuple-element.12.spin_ref, f32[2,2,8,128]{3,2,1,0:T(8,128)S(1)} %get-tuple-element.13.sign_ref, f32[128,16,128]{2,1,0:T(8,128)S(1)} %all_to_all.10.in_ref), custom_call_target="tpu_custom_call" | custom-call | flops 1677721600 | bytes 2097152 | tf_op jit(solution)/shard_map/pallas_call | solution.py:357
  50.2 15.0 %all_to_all.11 = f32[4,512,128]{2,1,0:T(8,128)S(1)} all-to-all(f32[4,512,128]{2,1,0:T(8,128)S(1)} %bitcast.7), channel_id=1, replica_groups=mesh['h3'=2,'hm'=4,'h0'=2,'z'=4,'x'=4,'core'=2] {'h0','h3'}, dimensions={0} | all-to-all | bytes 2097152 | tf_op jit(solution)/shard_map/all_to_all | solution.py:399
  65.3 1.1 %shard_map.39 = f32[32,4,16,128]{3,2,1,0:T(8,128)} custom-call(f32[2,3,2,6]{3,2,1,0:T(2,128)S(1)} %get-tuple-element.10.angles_ref, f32[4,4,8,128]{3,2,1,0:T(8,128)S(1)} %get-tuple-element.11.last_ref, f32[4,32,16,128]{3,2,1,0:T(8,128)S(1)} %bitcast.6), custom_call_target="tpu_custom_call" | custom-call | bytes 2097152 | tf_op jit(solution)/shard_map/pallas_call | solution.py:357

commit v7 on v5

--- a/solution.py
+++ b/solution.py
@@ -144,7 +144,8 @@
     chunks = [dot3(split(chunk), right0) for chunk in chunks]
     chunks = [dot3(left0, split(chunk)) * sign for chunk, sign in zip(chunks, signs0, strict=True)]
     chunks = [dot3(split(chunk), right1) for chunk in chunks]
-    return [dot3(left1, split(chunk)) * sign1 for chunk in chunks]
+    chunks = [dot3(left1, split(chunk)) for chunk in chunks]
+    return chunks if sign1 is None else [chunk * sign1 for chunk in chunks]
 
 
 def weighted(factors, values):
@@ -247,17 +248,19 @@
     for c in range(CHUNKS):
         chunks.append(mixed_chunk(enter[c], lambda k, half: held[halves(half), k]))
         signs0.append(outer_signs(edge, c))
-    chunks = chunk_layers(chunks, gates, signs0, chunk_sign(lambda b4, b7: edge))
+    chunks = chunk_layers(chunks, gates, signs0, None)
     for c, chunk in enumerate(chunks):
         for b0 in (0, 1):
             piece = of_chunk(chunk, b0)
             for at in range(16):
                 out_ref[spot(c, b0 * 16 + at)] = piece[at]
     for (b4, b7), factors in leave.items():
+        plain = [[factor * edge for factor in line] for line in factors]
+        turned = [[-factor for factor in line] for line in plain]
         for block in range(b4, BLOCKS, 2):
             tiles = [out_ref[spot(i, block), rows_of(b7)] for i in range(CHUNKS)]
             for o in range(CHUNKS):
-                out_ref[spot(o, block), rows_of(b7)] = weighted(factors[o], tiles)
+                out_ref[spot(o, block), rows_of(b7)] = weighted((turned if block >= 24 else plain)[o], tiles)
 
 
 def late():

time: 66.5 us -> 66.5 us (level)
  no operation moved by 1% of the time
where the time goes in v7:
time: 66.5 us; the launch traced here: 66.3 us
  blocking collectives  59.5 us (89%)
  Pallas kernels  6.78 us (10%)
    all_to_all x1, blocking collectives, on_device(): amps = lax.all_to_all(amps, GROUP, split_axis=0, concat_axis=0, tiled=True)  44.5 us
    all_to_all x1, blocking collectives, on_device(): lax.all_to_all(amps.reshape(CHUNKS, BLOCKS * ROWS, LANES), ('h3', 'h0'),...  15 us
    pallas_call x3, Pallas kernels, call(): pl.pallas_call(kernel, out_shape=out_shape, in_specs=specs or [VMEM] * le...  6.78 us

profile of v7, /device:TPU:16, one launch (start us, length us, event | category | flops | bytes accessed | tf_op | source)
XLA Modules:
  0.0 66.3 jit_solution(9476262755577954109)
XLA Ops:
  0.0 3.6 %shard_map.37 = (f32[128,16,128]{2,1,0:T(8,128)S(1)}, f32[2,3,2,6]{3,2,1,0:T(2,128)S(1)}, f32[4,4,8,128]{3,2,1,0:T(8,128)S(1)}, f32[2,2,8,128]{3,2,1,0:T(8,128)S(1)}, f32[4,4,8,128]{3,2,1,0:T(8,128)S(1)}) custom-call(f32[2,3,2,6]{3,2,1,0:T(2,128)} %bitcast.9, f32[1,2]{1,0:T(1,128)} %bitcast.10, f32[32,4,16,128]{3,2,1,0:T(8,128)} %bitcast.8), custom_call_target="tpu_custom_call" | custom-call | flops 1677721600 | bytes 2097152 | tf_op jit(solution)/shard_map/pallas_call | solution.py:356
  3.6 44.5 %all_to_all.10.in_ref = f32[128,16,128]{2,1,0:T(8,128)S(1)} all-to-all(f32[128,16,128]{2,1,0:T(8,128)S(1)} %get-tuple-element.14), channel_id=1, replica_groups=mesh['h3'=2,'hm'=4,'h0'=2,'z'=4,'x'=4,'core'=2] {'h0','x','core','h3','z'}, dimensions={0} | all-to-all | bytes 2097152 | tf_op jit(solution)/shard_map/all_to_all | solution.py:396
  48.1 2.2 %shard_map.38 = f32[4,32,16,128]{3,2,1,0:T(8,128)S(1)} custom-call(f32[2,3,2,6]{3,2,1,0:T(2,128)S(1)} %get-tuple-element.10.angles_ref, f32[4,4,8,128]{3,2,1,0:T(8,128)S(1)} %get-tuple-element.12.spin_ref, f32[2,2,8,128]{3,2,1,0:T(8,128)S(1)} %get-tuple-element.13.sign_ref, f32[128,16,128]{2,1,0:T(8,128)S(1)} %all_to_all.10.in_ref), custom_call_target="tpu_custom_call" | custom-call | flops 1677721600 | bytes 2097152 | tf_op jit(solution)/shard_map/pallas_call | solution.py:356
  50.2 15.0 %all_to_all.11 = f32[4,512,128]{2,1,0:T(8,128)S(1)} all-to-all(f32[4,512,128]{2,1,0:T(8,128)S(1)} %bitcast.7), channel_id=1, replica_groups=mesh['h3'=2,'hm'=4,'h0'=2,'z'=4,'x'=4,'core'=2] {'h3','h0'}, dimensions={0} | all-to-all | bytes 2097152 | tf_op jit(solution)/shard_map/all_to_all | solution.py:398
  65.3 1.1 %shard_map.39 = f32[32,4,16,128]{3,2,1,0:T(8,128)} custom-call(f32[2,3,2,6]{3,2,1,0:T(2,128)S(1)} %get-tuple-element.10.angles_ref, f32[4,4,8,128]{3,2,1,0:T(8,128)S(1)} %get-tuple-element.11.last_ref, f32[4,32,16,128]{3,2,1,0:T(8,128)S(1)} %bitcast.6), custom_call_target="tpu_custom_call" | custom-call | bytes 2097152 | tf_op jit(solution)/shard_map/pallas_call | solution.py:356
